TPU v7x, 256 devices: a whole 4x4x8 slice. The times are simulated.
256 devices in a mesh: comp: 32 (over y_hi, z, core), seq: 8 (over y_lo, x).
Axes of the slice: x: 4, y: 4 (y_hi: 2, y_lo: 2; y = y_hi * 2 + y_lo), z: 8, core: 2. Of those that a mesh axis runs over, the one named last changes fastest.
Arguments:
- comp_query: bfloat16 [32, 512, 16, 256], P('comp', None, 'seq'), may hold values from -180 to 180
- comp_key: bfloat16 [32, 512, 16, 256], P('comp', None, 'seq'), may hold values from -6 to 6
- comp_value: bfloat16 [32, 512, 16, 256], P('comp', None, 'seq'), may hold values from -6 to 6
- prompt_key: bfloat16 [512, 16, 256], P('seq'), may hold values from -7 to 7
- prompt_value: bfloat16 [512, 16, 256], P('seq'), may hold values from -6 to 6
- lam: float32 [16], P('seq'), may hold values from 0.2 to 0.8
- gain: float32 [16, 256], P('seq'), may hold values from 0.25 to 1.75
- cotangent: bfloat16 [32, 512, 16, 256], P('comp', None, 'seq'), may hold values from -6 to 6
- lengths: int32 [32], P('comp'), may hold values from 64 to 512, as said below
Outputs:
- grad_query: bfloat16 [32, 512, 16, 256], P('comp', None, 'seq')
- grad_key: bfloat16 [32, 512, 16, 256], P('comp', None, 'seq')
- grad_value: bfloat16 [32, 512, 16, 256], P('comp', None, 'seq')
- grad_prompt_key: bfloat16 [512, 16, 256], P(('comp', 'seq'))
- grad_prompt_value: bfloat16 [512, 16, 256], P(('comp', 'seq'))
Inputs may be any that keep to these rules, and one draw needn't show every extreme that they name: `lengths`: some completion has all 512 tokens live.
All inputs are finite; a program needn't handle non-finite values.
Results may differ from a plain program's by a relative error of at most 0.017.
Values may be sent and summed in bfloat16 or wider, within the bound.
A program may use at most 64 MiB of HBM per device.

v0:
```python
import jax
import jax.numpy as jnp
from jax import lax
from jax.sharding import PartitionSpec as P


def pair_dot(left, right, left_dim, right_dim):
    return lax.dot_general(
        left, right, (((left_dim,), (right_dim,)), ((), ())), preferred_element_type=jnp.float32
    )


def head_terms(queries, all_keys, all_values, grad_out, weight_two, norm_gain, live_rows, visible):
    half_width = queries.shape[1] // 2
    score_scale = float(half_width) ** (-0.5)
    first_query, second_query = (queries[:, :half_width], queries[:, half_width:])
    first_key, second_key = (all_keys[:, :half_width], all_keys[:, half_width:])

    def softmax_rows(scores):
        scores = jnp.where(visible, scores, -1e30)
        peak = jnp.max(scores, axis=1, keepdims=True)
        expo = jnp.exp(scores - peak)
        return expo / jnp.sum(expo, axis=1, keepdims=True)

    map_one = softmax_rows(score_scale * pair_dot(first_query, first_key, 1, 1))
    map_two = softmax_rows(score_scale * pair_dot(second_query, second_key, 1, 1))
    mixed = (map_one - weight_two * map_two).astype(jnp.bfloat16)
    attn = pair_dot(mixed, all_values, 1, 0)
    recip = lax.rsqrt(jnp.mean(attn * attn, axis=1, keepdims=True) + 1e-05)
    normed_grad = (
        jnp.where(live_rows[:, None], grad_out.astype(jnp.float32), 0.0) * norm_gain[None, :]
    )
    inner = jnp.mean(normed_grad * attn, axis=1, keepdims=True)
    d_attn = (recip * (normed_grad - attn * recip * recip * inner)).astype(jnp.bfloat16)
    d_mixed = pair_dot(d_attn, all_values, 1, 1)
    sum_one = jnp.sum(map_one * d_mixed, axis=1, keepdims=True)
    sum_two = jnp.sum(map_two * d_mixed, axis=1, keepdims=True)
    d_score_one = (map_one * (d_mixed - sum_one)).astype(jnp.bfloat16)
    d_score_two = (-weight_two * map_two * (d_mixed - sum_two)).astype(jnp.bfloat16)
    grad_q = score_scale * jnp.concatenate(
        [pair_dot(d_score_one, first_key, 1, 0), pair_dot(d_score_two, second_key, 1, 0)], axis=1
    )
    grad_k = score_scale * jnp.concatenate(
        [pair_dot(d_score_one, first_query, 0, 0), pair_dot(d_score_two, second_query, 0, 0)],
        axis=1,
    )
    grad_v = pair_dot(mixed, d_attn, 0, 0)
    return (grad_q, grad_k, grad_v)


def shards(
    comp_query, comp_key, comp_value, prompt_key, prompt_value, lam, gain, cotangent, lengths
):
    prompt_keys, prompt_values = (
        lax.all_to_all(prompt_key, "seq", split_axis=1, concat_axis=0, tiled=True),
        lax.all_to_all(prompt_value, "seq", split_axis=1, concat_axis=0, tiled=True),
    )
    prompt_len = prompt_keys.shape[0]
    row_count = comp_query.shape[1]
    local_heads = comp_query.shape[2]
    all_keys = jnp.concatenate([prompt_keys, comp_key[0]], axis=0)
    all_values = jnp.concatenate([prompt_values, comp_value[0]], axis=0)
    key_total = all_keys.shape[0]
    block_rows = min(512, row_count)
    length = lengths[0]
    trip_count = row_count // block_rows
    key_places = jnp.arange(key_total, dtype=jnp.int32) - prompt_len
    query_grads, key_grads, value_grads = ([], [], [])
    prompt_key_parts, prompt_value_parts = ([], [])
    for head_index in range(local_heads):
        head_query = comp_query[0, :, head_index]
        head_keys = all_keys[:, head_index]
        head_values = all_values[:, head_index]
        head_grad = cotangent[0, :, head_index]

        def block_step(block_index, totals):
            first_row = block_index * block_rows
            places = first_row + jnp.arange(block_rows, dtype=jnp.int32)
            live_rows = places < length
            visible = key_places[None, :] <= places[:, None]
            grad_q, grad_k, grad_v = head_terms(
                head_query,
                head_keys,
                head_values,
                head_grad,
                lam[head_index],
                gain[head_index],
                live_rows,
                visible,
            )
            return (grad_q, totals[1] + grad_k, totals[2] + grad_v)

        start_totals = (
            jnp.zeros((row_count, head_query.shape[1]), jnp.float32),
            jnp.zeros((key_total, head_keys.shape[1]), jnp.float32),
            jnp.zeros((key_total, head_values.shape[1]), jnp.float32),
        )
        grad_q, grad_k, grad_v = lax.fori_loop(0, trip_count, block_step, start_totals)
        query_grads.append(grad_q)
        key_grads.append(grad_k[prompt_len:])
        value_grads.append(grad_v[prompt_len:])
        prompt_key_parts.append(grad_k[:prompt_len])
        prompt_value_parts.append(grad_v[:prompt_len])
    partial_key = jnp.stack(prompt_key_parts, axis=1)
    partial_value = jnp.stack(prompt_value_parts, axis=1)
    summed_key, summed_value = (
        lax.psum_scatter(partial_key, "comp", scatter_dimension=0, tiled=True),
        lax.psum_scatter(partial_value, "comp", scatter_dimension=0, tiled=True),
    )
    owned_key, owned_value = (
        lax.all_to_all(
            summed_key.astype(jnp.bfloat16), "seq", split_axis=0, concat_axis=1, tiled=True
        ).astype(summed_key.dtype),
        lax.all_to_all(
            summed_value.astype(jnp.bfloat16), "seq", split_axis=0, concat_axis=1, tiled=True
        ).astype(summed_value.dtype),
    )
    grad_query = jnp.stack(query_grads, axis=1)[None].astype(jnp.bfloat16)
    grad_key = jnp.stack(key_grads, axis=1)[None].astype(jnp.bfloat16)
    grad_value = jnp.stack(value_grads, axis=1)[None].astype(jnp.bfloat16)
    return (
        grad_query,
        grad_key,
        grad_value,
        owned_key.astype(jnp.bfloat16),
        owned_value.astype(jnp.bfloat16),
    )


def solution(mesh):
    in_specs = (
        P("comp", None, "seq", None),
        P("comp", None, "seq", None),
        P("comp", None, "seq", None),
        P("seq", None, None),
        P("seq", None, None),
        P("seq"),
        P("seq", None),
        P("comp", None, "seq", None),
        P("comp"),
    )
    out_specs = (
        P("comp", None, "seq", None),
        P("comp", None, "seq", None),
        P("comp", None, "seq", None),
        P(("comp", "seq"), None, None),
        P(("comp", "seq"), None, None),
    )
    return jax.shard_map(shards, mesh=mesh, in_specs=in_specs, out_specs=out_specs, check_vma=False)
```

profile of v0, /device:TPU:2, one launch (start us, length us, event | category | flops | bytes accessed | tf_op | source)
XLA Modules:
  0.0 241.4 jit_solution(4977528223593420519)
XLA Ops:
  7.2 2.1 copy.75
  9.3 6.0 %all-to-all-start = ((bf16[64,16,256]{2,0,1:T(8,128)(2,1)}), bf16[64,16,256]{2,0,1:T(8,128)(2,1)S(1)}, u32[]{:S(2)}, u32[]{:S(2)}) async-start(bf16[64,16,256]{2,0,1:T(8,128)(2,1)} %copy.75), calls=%async_computation | async-start | bytes 1048576 | tf_op jit(solution)/shard_map/all_to_all | solution.py:55
  21.3 1.3 copy.104
  25.4 5.7 %all-to-all-start.1 = ((bf16[64,16,256]{2,0,1:T(8,128)(2,1)}), bf16[64,16,256]{2,0,1:T(8,128)(2,1)S(1)}, u32[]{:S(2)}, u32[]{:S(2)}) async-start(bf16[64,16,256]{2,0,1:T(8,128)(2,1)} %copy.79), calls=%async_computation.1 | async-start | bytes 1048576 | tf_op jit(solution)/shard_map/all_to_all | solution.py:56
  31.2 1.8 fusion.68
  33.0 1.8 fusion.69
  35.2 1.8 fusion.71
  37.0 2.4 %all-to-all-done.1 = bf16[64,16,256]{2,0,1:T(8,128)(2,1)S(1)} async-done(((bf16[64,16,256]{2,0,1:T(8,128)(2,1)}), bf16[64,16,256]{2,0,1:T(8,128)(2,1)S(1)}, u32[]{:S(2)}, u32[]{:S(2)}) %all-to-all-start.1) | async-done | bytes 524320 | tf_op jit(solution)/shard_map/all_to_all | solution.py:56
  39.8 1.2 copy-done
  41.4 1.5 subtract_convert_fusion.1
  43.4 1.0 copy-done.1
  45.4 1.4 subtract_convert_fusion
  48.1 1.0 multiply_reduce_fusion.1
  49.1 1.0 multiply_convert_fusion.1
  50.5 1.3 fusion.45
  51.8 1.1 convolution_bitcast_fusion
  52.8 1.3 fusion.42
  55.6 1.0 multiply_convert_fusion.3
  56.6 1.0 convolution_bitcast_fusion.3
  58.4 1.1 pad_maximum_fusion.1
  63.2 145.8 %all-reduce.2 = bf16[512,2,256]{2,1,0:T(2,128)(2,1)} all-reduce(f32[512,2,256]{2,1,0:T(2,128)S(1)} %copy.93), channel_id=2, replica_groups=mesh['comp'=32,'seq'=8] {'comp'}, use_global_device_ids=true, to_apply=%region_16.17.clone | all-reduce | flops 262144 | bytes 1572864
  209.1 1.3 dynamic-slice_convert_fusion
  210.4 5.7 %all-to-all-start.2 = ((bf16[16,2,256]{2,1,0:T(2,128)(2,1)}), bf16[16,2,256]{2,1,0:T(2,128)(2,1)S(1)}, u32[]{:S(2)}, u32[]{:S(2)}) async-start(bf16[16,2,256]{2,1,0:T(2,128)(2,1)} %dynamic-slice_convert_fusion), calls=%async_computation.2 | async-start | bytes 32768 | tf_op jit(solution)/shard_map/all_to_all | solution.py:111
  216.1 1.0 fusion.28
  217.6 1.1 fusion.33
  218.6 1.1 fusion.32
  219.8 1.1 fusion.31
  220.8 1.1 fusion.30
  223.4 5.7 %all-to-all-start.3 = ((bf16[16,2,256]{2,1,0:T(2,128)(2,1)}), bf16[16,2,256]{2,1,0:T(2,128)(2,1)S(1)}, u32[]{:S(2)}, u32[]{:S(2)}) async-start(bf16[16,2,256]{2,1,0:T(2,128)(2,1)} %copy.95), calls=%async_computation.4 | async-start | bytes 32768 | tf_op jit(solution)/shard_map/all_to_all | solution.py:114
  229.2 1.3 copy.99
  230.5 1.1 copy.97
  231.6 1.1 copy.98
  (116 shorter events, 20.2 us)
Async XLA Ops:
  7.2 8.8 %copy-start.28 = (f32[2]{0:T(128)S(1)}, f32[2]{0:T(128)}, u32[]{:S(2)}) copy-start(f32[2]{0:T(128)} %param.14) | copy-start | bytes 28
  7.2 10.7 %copy-start.22 = (bf16[1,512,2,256]{3,2,1,0:T(2,128)(2,1)S(1)}, bf16[1,512,2,256]{3,2,1,0:T(2,128)(2,1)}, u32[]{:S(2)}) copy-start(bf16[1,512,2,256]{3,2,1,0:T(2,128)(2,1)} %param.10) | copy-start | bytes 1572868
  7.2 10.8 %copy-start.23 = (bf16[1,512,2,256]{3,2,1,0:T(2,128)(2,1)S(1)}, bf16[1,512,2,256]{3,2,1,0:T(2,128)(2,1)}, u32[]{:S(2)}) copy-start(bf16[1,512,2,256]{3,2,1,0:T(2,128)(2,1)} %param.11) | copy-start | bytes 1572868
  7.2 11.6 %copy-start.24 = (bf16[64,16,256]{2,1,0:T(8,128)(2,1)S(1)}, bf16[64,16,256]{2,1,0:T(8,128)(2,1)}, u32[]{:S(2)}) copy-start(bf16[64,16,256]{2,1,0:T(8,128)(2,1)} %param.13) | copy-start | bytes 1572868
  9.3 10.5 %copy-start.7 = (bf16[1,512,2,256]{3,2,1,0:T(2,128)(2,1)S(1)}, bf16[1,512,2,256]{3,2,1,0:T(2,128)(2,1)}, u32[]{:S(2)}) copy-start(bf16[1,512,2,256]{3,2,1,0:T(2,128)(2,1)} %param.9) | copy-start | bytes 1572868
  9.3 16.0 %all-to-all-start = ((bf16[64,16,256]{2,0,1:T(8,128)(2,1)}), bf16[64,16,256]{2,0,1:T(8,128)(2,1)S(1)}, u32[]{:S(2)}, u32[]{:S(2)}) async-start(bf16[64,16,256]{2,0,1:T(8,128)(2,1)} %copy.75), calls=%async_computation | async-start | bytes 1048576 | tf_op jit(solution)/shard_map/all_to_all | solution.py:55
  18.0 2.6 %copy-start.8 = (bf16[1,512,2,256]{3,2,1,0:T(2,128)(2,1)S(1)}, bf16[1,512,2,256]{3,2,1,0:T(2,128)(2,1)}, u32[]{:S(2)}) copy-start(bf16[1,512,2,256]{3,2,1,0:T(2,128)(2,1)} %param.16) | copy-start | bytes 1572868
  20.5 2.8 %copy-start.29 = (u32[256]{0:T(256)S(1)}, u32[256]{0:T(256)}, u32[]{:S(2)}) copy-start(u32[256]{0:T(256)} %constant.63) | copy-start | bytes 3076
  20.5 4.0 %copy-start.27 = (f32[2,256]{1,0:T(2,128)S(1)}, f32[2,256]{1,0:T(2,128)}, u32[]{:S(2)}) copy-start(f32[2,256]{1,0:T(2,128)} %param.15) | copy-start | bytes 6148
  25.4 7.6 %copy-start.20 = (bf16[512,256]{1,0:T(8,128)(2,1)}, bf16[512,256]{1,0:T(8,128)(2,1)S(1)}, u32[]{:S(2)}) copy-start(bf16[512,256]{1,0:T(8,128)(2,1)S(1)} %get-tuple-element.136) | copy-start | bytes 786436
  25.4 14.1 %all-to-all-start.1 = ((bf16[64,16,256]{2,0,1:T(8,128)(2,1)}), bf16[64,16,256]{2,0,1:T(8,128)(2,1)S(1)}, u32[]{:S(2)}, u32[]{:S(2)}) async-start(bf16[64,16,256]{2,0,1:T(8,128)(2,1)} %copy.79), calls=%async_computation.1 | async-start | bytes 1048576 | tf_op jit(solution)/shard_map/all_to_all | solution.py:56
  31.1 190.9 %reduce-scatter.2.cloned.1.call-start = ((), (), s32[]{:S(2)}) async-start(), calls=%async_computation.5 | async-start | bytes 1081344 | tf_op jit(solution)/shard_map/reduce_scatter | solution.py:108
  31.2 3.6 %copy-start.14 = (bf16[1024,256]{1,0:T(8,128)(2,1)}, bf16[1024,256]{1,0:T(8,128)(2,1)S(1)}, u32[]{:S(2)}) copy-start(bf16[1024,256]{1,0:T(8,128)(2,1)S(1)} %get-tuple-element.114) | copy-start | bytes 1572868
  31.2 4.0 %copy-start.11 = (bf16[1024,256]{1,0:T(8,128)(2,1)}, bf16[1024,256]{1,0:T(8,128)(2,1)S(1)}, u32[]{:S(2)}) copy-start(bf16[1024,256]{1,0:T(8,128)(2,1)S(1)} %get-tuple-element.113) | copy-start | bytes 1572868
  33.0 1.8 copy-start.17
  39.4 1.6 copy-start
  41.4 1.5 copy-start.25
  41.4 1.5 copy-start.26
  42.8 1.6 copy-start.1
  42.9 2.2 copy-start.2
  48.1 10.2 %copy-start.3 = (f32[1024,256]{1,0:T(8,128)}, f32[1024,256]{1,0:T(8,128)S(1)}, u32[]{:S(2)}) copy-start(f32[1024,256]{1,0:T(8,128)S(1)} %fusion.73) | copy-start | bytes 3145732
  49.1 1.0 copy-start.15
  49.1 1.4 copy-start.21
  54.6 3.8 %copy-start.4 = (f32[1024,256]{1,0:T(8,128)}, f32[1024,256]{1,0:T(8,128)S(1)}, u32[]{:S(2)}) copy-start(f32[1024,256]{1,0:T(8,128)S(1)} %fusion.72) | copy-start | bytes 3145732
  55.5 2.1 copy-start.18
  58.4 1.2 copy-start.9
  58.4 1.6 copy-start.10
  60.1 1.4 copy-start.5
  63.2 153.9 %copy-start.13 = (bf16[1024,256]{1,0:T(8,128)(2,1)S(1)}, bf16[1024,256]{1,0:T(8,128)(2,1)}, u32[]{:S(2)}) copy-start(bf16[1024,256]{1,0:T(8,128)(2,1)} %copy-done.11) | copy-start | bytes 1572868
  63.2 154.3 %copy-start.16 = (f32[512,1,128]{0,2,1:T(8,128)S(1)}, f32[512,1,128]{0,2,1:T(8,128)}, u32[]{:S(2)}) copy-start(f32[512,1,128]{0,2,1:T(8,128)} %convolution_bitcast_fusion.3) | copy-start | bytes 786436
  210.4 13.0 %all-to-all-start.2 = ((bf16[16,2,256]{2,1,0:T(2,128)(2,1)}), bf16[16,2,256]{2,1,0:T(2,128)(2,1)S(1)}, u32[]{:S(2)}, u32[]{:S(2)}) async-start(bf16[16,2,256]{2,1,0:T(2,128)(2,1)} %dynamic-slice_convert_fusion), calls=%async_computation.2 | async-start | bytes 32768 | tf_op jit(solution)/shard_map/all_to_all | solution.py:111
  223.4 10.5 %all-to-all-start.3 = ((bf16[16,2,256]{2,1,0:T(2,128)(2,1)}), bf16[16,2,256]{2,1,0:T(2,128)(2,1)S(1)}, u32[]{:S(2)}, u32[]{:S(2)}) async-start(bf16[16,2,256]{2,1,0:T(2,128)(2,1)} %copy.95), calls=%async_computation.4 | async-start | bytes 32768 | tf_op jit(solution)/shard_map/all_to_all | solution.py:114
  (3 other events, 3.0 us)
Sparse Core Ops, SparseCore 0:
  59.7 116.4 reduce-scatter.1
where the time goes:
time: 242 us; the launch traced here: 241 us
  blocking collectives  146 us (60%)
  local copies, waits for them, and re-layouts  26 us (11%)
  starting transfers between devices  23.2 us (10%)
  between operations  17.2 us (7%)
  matrix products  16.2 us (7%)
  other arithmetic  9.91 us (4%)
  waiting for transfers between devices  3.08 us (1%)
    unnamed x1, blocking collectives  146 us
    dot_general x18, matrix products, pair_dot(): lax.dot_general(left, right, (((left_dim,), (right_dim,)), ((), ())), pre...  16.2 us
    unnamed x71, local copies, waits for them, and re-layouts  15.5 us
    all_to_all x1, starting transfers between devices, shards(): lax.all_to_all(prompt_key, 'seq', split_axis=1, concat_axis=0, tiled=True)  5.97 us
    all_to_all x1, starting transfers between devices, shards(): lax.all_to_all(summed_key.astype(jnp.bfloat16), 'seq', split_axis=0, conc...  5.74 us
    all_to_all x1, starting transfers between devices, shards(): lax.all_to_all(summed_value.astype(jnp.bfloat16), 'seq', split_axis=0, co...  5.74 us
    all_to_all x1, starting transfers between devices, shards(): lax.all_to_all(prompt_value, 'seq', split_axis=1, concat_axis=0, tiled=True)  5.7 us
  transfers between devices with their start and end apart: 5, of which 2 were waited for; matrix products, arithmetic and copies ran while one was open for 11% of the time, Pallas kernels for 0%

commit v1 on v0

v1 whole, which is shorter than its diff:
```python
import math

import jax
import jax.numpy as jnp
from jax import lax
from jax.experimental import pallas as pl
from jax.experimental.pallas import tpu as pltpu
from jax.sharding import PartitionSpec as P

F32, BF16 = jnp.float32, jnp.bfloat16
MESH = pl.DeviceIdType.MESH
SCALE = 128**-0.5
EXPO = SCALE * math.log2(math.e)
ROWS = 32
PROMPT_CHUNKS = ((0, 256, 0), (256, 256, 0))
COMP_CHUNKS = ((512, 256, 0), (768, 256, 256))
CHUNKS = PROMPT_CHUNKS + COMP_CHUNKS
SEQ_OFFSETS = ((1, 2), (0, 2), (1, 1), (1, 3), (0, 1), (0, 3), (1, 0))
COMP_OFFSETS = tuple((dy, dz) for dz in (4, 3, 5, 2, 6, 1, 7, 0) for dy in (1, 0) if (dy, dz) != (0, 0))


def nt(a, b):
    return lax.dot_general(a, b, (((1,), (1,)), ((), ())), preferred_element_type=F32)


def nn(a, b):
    return lax.dot_general(a, b, (((1,), (0,)), ((), ())), preferred_element_type=F32)


def iota(shape, dim):
    return lax.broadcasted_iota(jnp.int32, shape, dim)


def one_hot(hits):
    return jnp.where(hits, 1.0, 0.0).astype(BF16)


def half(i):
    return slice(i * 128, (i + 1) * 128)


def fold(x, op):
    return op(x.reshape(x.shape[0] // 8, 8, x.shape[1]), axis=0)


def merge(acc, part, first, op):
    if acc is None:
        return part
    if first:
        return jnp.concatenate([acc[:, :first], op(acc[:, first:], part)], axis=1)
    return op(acc, part)


def kernel(
    query_in, key_in, value_in, cot_in, pkey_in, pvalue_in, lam_in, gain_in, length_in,
    query_out, key_out, value_out, pkey_out, pvalue_out,
    qx, kx, vx, cx, pkx, pvx, lam, gain, length,
    prompt_send, kn, vn, qn, cn, kT, vT, cT,
    s1, s2, dm, mixT, ds1, ds2, dT,
    gq, gk, gv, gpack, part, sibling, zsend, zrecv, fsend, frecv, fout,
    in_sem, out_sem, ps_sem, pr_sem, fs_sem, fr_sem, cs_sem, cr_sem, zs_sem, zr_sem, as_sem, ar_sem,
):
    c, s = lax.axis_index("comp"), lax.axis_index("seq")
    core = lax.rem(c, 2)
    z = lax.rem(lax.div(c, 2), 8)
    y_hi = lax.div(c, 16)
    x = lax.rem(s, 4)
    y_lo = lax.div(s, 4)
    mate = (c + 1 - 2 * core, s)

    def seq_to(dy, dx):
        return lax.rem(y_lo + dy, 2) * 4 + lax.rem(x + dx, 4)

    def gather_to(dy, dx):
        comp = lax.rem(c + 16 * core, 32) if dy else c
        return comp, seq_to(dy, dx)

    def comp_at(dy, dz):
        return lax.rem(y_hi + dy, 2) * 8 + lax.rem(z + dz, 8)

    pairs = (
        (pkey_in, pkx), (pvalue_in, pvx), (query_in, qx), (key_in, kx), (value_in, vx), (cot_in, cx),
        (gain_in, gain), (lam_in, lam), (length_in, length),
    )
    loads = [pltpu.make_async_copy(src, dst, in_sem.at[i]) for i, (src, dst) in enumerate(pairs)]
    for load in loads:
        load.start()

    barrier = pltpu.get_barrier_semaphore()
    greet = [mate]
    greet += [gather_to(dy, dx) for dy, dx in SEQ_OFFSETS]
    greet += [(c, seq_to(dy, dx)) for dy, dx in SEQ_OFFSETS]
    greet += [(comp_at(dy, dz) * 2 + core, s) for dy, dz in COMP_OFFSETS]
    for peer in greet:
        pl.semaphore_signal(barrier, inc=1, device_id=peer, device_id_type=MESH)

    rows, cols = iota((256, 256), 0), iota((256, 256), 1)
    by_head = one_hot(cols == lax.rem(rows, 16) * 16 + lax.div(rows, 16))

    def repack(which, packed, keep):
        for b in range(4):
            got = nn(by_head, packed[b * 256 : (b + 1) * 256, :]).astype(BF16)
            for head in range(16):
                prompt_send[which, head // 2, head % 2, b * 16 : (b + 1) * 16, :] = got[head * 16 : (head + 1) * 16]
        for h in range(2):
            keep[h, pl.ds(pl.multiple_of(s * 64, 64), 64), :] = prompt_send[which, s, h]

    def prompt_copy(which, h, i, dy, dx):
        dst = (kn, vn)[which]
        here = pl.ds(pl.multiple_of(s * 64 + core * 32, 32), 32)
        return pltpu.make_async_remote_copy(
            prompt_send.at[which, seq_to(dy, dx), h, pl.ds(pl.multiple_of(core * 32, 32), 32)],
            dst.at[h, here],
            ps_sem.at[which, h, i],
            pr_sem.at[which, h, i],
            device_id=gather_to(dy, dx),
            device_id_type=MESH,
        )

    def forward_copy(which, h, i, dy, dx):
        dst = (kn, vn)[which]
        origin = lax.rem(y_lo + dy, 2) * 4 + lax.rem(x + 4 - dx, 4)
        there = pl.ds(pl.multiple_of(origin * 64 + core * 32, 32), 32)
        return pltpu.make_async_remote_copy(
            dst.at[h, there], dst.at[h, there], fs_sem.at[which, h, i], fr_sem.at[which, h, i],
            device_id=mate, device_id_type=MESH,
        )

    def prompt_start(which, h):
        for i, (dy, dx) in enumerate(SEQ_OFFSETS):
            prompt_copy(which, h, i, dy, dx).start()

    def prompt_forward(which, h):
        for i, (dy, dx) in reversed(tuple(enumerate(SEQ_OFFSETS))):
            prompt_copy(which, h, i, dy, dx).wait_recv()
            forward_copy(which, h, i, dy, dx).start()

    def prompt_arrived(which, h):
        for i, (dy, dx) in enumerate(SEQ_OFFSETS):
            forward_copy(which, h, i, dy, dx).wait_recv()

    loads[0].wait()
    repack(0, pkx, kn)
    pl.semaphore_wait(barrier, len(greet))
    prompt_start(0, 0)
    loads[1].wait()
    repack(1, pvx, vn)
    prompt_start(1, 0)
    prompt_start(0, 1)
    prompt_start(1, 1)

    apart = one_hot(cols == lax.rem(rows, 64) * 4 + lax.rem(lax.div(rows, 64), 2) * 2 + lax.div(rows, 128))
    together = one_hot(rows == lax.rem(cols, 64) * 4 + lax.rem(lax.div(cols, 64), 2) * 2 + lax.div(cols, 128))

    def unpack(first, second, first_to, second_to, first_row, second_row):
        for b in range(8):
            block = slice(b * 256, (b + 1) * 256)
            got = nn(apart, jnp.concatenate([first[block, :], second[block, :]], axis=1)).astype(BF16)
            for h in range(2):
                for i in range(2):
                    r = (h * 2 + i) * 64
                    t = b * 64
                    first_to[h, first_row + t : first_row + t + 64, half(i)] = got[r : r + 64, :128]
                    second_to[h, second_row + t : second_row + t + 64, half(i)] = got[r : r + 64, 128:]

    def turn(src, dst, h, first, last):
        for b in range(first, last, 256):
            dst[h, :, b : b + 256] = src[h, b : b + 256, :].T

    def scores(h, chunks, tops):
        for k0, n, q0 in chunks:
            for i, to in ((0, s1), (1, s2)):
                val = nt(kn[h, k0 : k0 + n, half(i)], qn[h, q0:, half(i)])
                for r in range(0, n, ROWS):
                    bit = val[r : r + ROWS]
                    if k0 >= 512:
                        seen = iota(bit.shape, 0) + (k0 - 512 + r) <= iota(bit.shape, 1) + q0
                        bit = jnp.where(seen, bit, -1e30)
                    to[h, k0 + r : k0 + r + ROWS, q0:] = bit
                    tops[i] = merge(tops[i], fold(bit, jnp.max), q0, jnp.maximum)

    def softmax(h, tops):
        sums = [None, None]
        for i, to in ((0, s1), (1, s2)):
            top = jnp.max(tops[i], axis=0, keepdims=True) * EXPO
            for k0, n, q0 in CHUNKS:
                for r in range(k0, k0 + n, ROWS):
                    e = jnp.exp2(to[h, r : r + ROWS, q0:] * EXPO - top[:, q0:])
                    to[h, r : r + ROWS, q0:] = e
                    sums[i] = merge(sums[i], fold(e, jnp.sum), q0, jnp.add)
        return [jnp.sum(total, axis=0, keepdims=True) for total in sums]

    def forward(h, sums):
        one, two = 1.0 / sums[0], lam[h] / sums[1]
        attn = None
        for k0, n, q0 in CHUNKS:
            for r in range(k0, k0 + n, ROWS):
                a1 = s1[h, r : r + ROWS, q0:] * one[:, q0:]
                a2 = s2[h, r : r + ROWS, q0:] * two[:, q0:]
                s1[h, r : r + ROWS, q0:] = a1
                s2[h, r : r + ROWS, q0:] = a2
                mixT[h, r : r + ROWS, q0:] = (a1 - a2).astype(BF16)
            attn = merge(attn, nn(vT[h, :, k0 : k0 + n], mixT[h, k0 : k0 + n, q0:]), q0, jnp.add)
        recip = lax.rsqrt(jnp.sum(attn * attn, axis=0, keepdims=True) * (1.0 / 256) + 1e-5)
        live = iota((1, 512), 1) < length[0]
        grad = jnp.where(live, cT[h].astype(F32), 0.0) * gains[:, h : h + 1]
        inner = jnp.sum(grad * attn, axis=0, keepdims=True) * (1.0 / 256)
        dT[h] = (recip * (grad - attn * (recip * recip * inner))).astype(BF16)

    def to_part(unit, k0, val, columns):
        for r in range(0, val.shape[0], 16):
            block = (k0 + r) // 16
            part[unit, block % 2, block // 2, :, columns] = val[r : r + 16].astype(BF16)

    def value_grads(h, chunks):
        for k0, n, q0 in chunks:
            val = nt(mixT[h, k0 : k0 + n, q0:], dT[h, :, q0:])
            if k0 < 512:
                to_part(2 * h, k0, val, slice(0, 256))
            else:
                gv[h, k0 - 512 : k0 - 512 + n, :] = val.astype(BF16)

    def key_grads(h, chunks):
        for k0, n, q0 in chunks:
            for i, ds in ((0, ds1), (1, ds2)):
                val = nn(ds[h, k0 : k0 + n, q0:], qn[h, q0:, half(i)]) * SCALE
                if k0 < 512:
                    to_part(2 * h + 1, k0, val, half(i))
                else:
                    gk[h, k0 - 512 : k0 - 512 + n, half(i)] = val.astype(BF16)

    def query_grads(h):
        for i, ds in ((0, ds1), (1, ds2)):
            total = None
            for k0, n, q0 in CHUNKS:
                total = merge(total, nn(kT[h, half(i), k0 : k0 + n], ds[h, k0 : k0 + n, q0:]), q0, jnp.add)
            gq[h, :, half(i)] = (total * SCALE).astype(BF16).T

    def row_sums(h):
        sums = [None, None]
        for k0, n, q0 in CHUNKS:
            val = nn(vn[h, k0 : k0 + n, :], dT[h, :, q0:])
            for r in range(0, n, ROWS):
                bit = val[r : r + ROWS]
                dm[k0 + r : k0 + r + ROWS, q0:] = bit
                for i, a in ((0, s1), (1, s2)):
                    prod = fold(a[h, k0 + r : k0 + r + ROWS, q0:] * bit, jnp.sum)
                    sums[i] = merge(sums[i], prod, q0, jnp.add)
        e1, e2 = [jnp.sum(total, axis=0, keepdims=True) for total in sums]
        return e1, e2 / lam[h]

    def score_grads(h, e1, e2, chunks):
        for k0, n, q0 in chunks:
            for r in range(k0, k0 + n, ROWS):
                bit = dm[r : r + ROWS, q0:]
                ds1[h, r : r + ROWS, q0:] = (s1[h, r : r + ROWS, q0:] * (bit - e1[:, q0:])).astype(BF16)
                ds2[h, r : r + ROWS, q0:] = (s2[h, r : r + ROWS, q0:] * (e2[:, q0:] - bit)).astype(BF16)

    def mate_copy(unit):
        return pltpu.make_async_remote_copy(
            part.at[unit, 1 - core], sibling.at[unit], cs_sem.at[unit], cr_sem.at[unit],
            device_id=mate, device_id_type=MESH,
        )

    def chip_copy(unit, i, dy, dz):
        return pltpu.make_async_remote_copy(
            zsend.at[unit, comp_at(dy, dz)], zrecv.at[unit, i], zs_sem.at[unit, i], zr_sem.at[unit, i],
            device_id=(comp_at(dy, dz) * 2 + core, s), device_id_type=MESH,
        )

    def send_chips(unit):
        mate_copy(unit).wait_recv()
        for b in range(16):
            zsend[unit, b] = (part[unit, core, b].astype(F32) + sibling[unit, b].astype(F32)).astype(BF16)
        for i, (dy, dz) in enumerate(COMP_OFFSETS):
            chip_copy(unit, i, dy, dz).start()

    def sum_chips(unit):
        total = zsend[unit, comp_at(0, 0)].astype(F32)
        for i, (dy, dz) in enumerate(COMP_OFFSETS):
            chip_copy(unit, i, dy, dz).wait_recv()
            total = total + zrecv[unit, i].astype(F32)
        return total

    loads[2].wait()
    loads[3].wait()
    unpack(qx, kx, qn, kn, 0, 512)
    tops = ([None, None], [None, None])
    scores(0, COMP_CHUNKS, tops[0])
    loads[4].wait()
    loads[5].wait()
    unpack(vx, cx, vn, cn, 512, 0)
    for load in loads[6:]:
        load.wait()
    gains = jnp.concatenate([gain[...], jnp.zeros((6, 256), F32)], axis=0).T
    for h in range(2):
        turn(cn, cT, h, 0, 512)
        turn(kn, kT, h, 512, 1024)
        turn(vn, vT, h, 512, 1024)
    scores(1, COMP_CHUNKS, tops[1])
    prompt_forward(0, 0)
    prompt_arrived(0, 0)
    scores(0, PROMPT_CHUNKS, tops[0])
    prompt_forward(1, 0)
    turn(kn, kT, 0, 0, 512)
    sums = softmax(0, tops[0])
    prompt_arrived(1, 0)
    turn(vn, vT, 0, 0, 512)
    prompt_forward(0, 1)
    forward(0, sums)
    value_grads(0, PROMPT_CHUNKS)
    mate_copy(0).start()
    prompt_forward(1, 1)
    e1, e2 = row_sums(0)
    send_chips(0)
    score_grads(0, e1, e2, PROMPT_CHUNKS)
    key_grads(0, PROMPT_CHUNKS)
    mate_copy(1).start()
    prompt_arrived(0, 1)
    scores(1, PROMPT_CHUNKS, tops[1])
    send_chips(1)
    score_grads(0, e1, e2, COMP_CHUNKS)
    sums = softmax(1, tops[1])
    prompt_arrived(1, 1)
    turn(vn, vT, 1, 0, 512)
    forward(1, sums)
    value_grads(1, PROMPT_CHUNKS)
    mate_copy(2).start()
    e1, e2 = row_sums(1)
    send_chips(2)
    score_grads(1, e1, e2, PROMPT_CHUNKS)
    key_grads(1, PROMPT_CHUNKS)
    mate_copy(3).start()
    score_grads(1, e1, e2, COMP_CHUNKS)
    turn(kn, kT, 1, 0, 512)
    send_chips(3)

    stores = []

    def hand_out(i, packed, out):
        for b in range(8):
            bits = [packed[h, b * 64 : (b + 1) * 64, half(i)] for h in range(2) for i in range(2)]
            gpack[i, b * 256 : (b + 1) * 256, :] = nn(together, jnp.concatenate(bits, axis=0)).astype(BF16)
        store = pltpu.make_async_copy(gpack.at[i], out, out_sem.at[i])
        store.start()
        stores.append(store)

    for h in range(2):
        value_grads(h, COMP_CHUNKS)
    hand_out(0, gv, value_out)
    for h in range(2):
        key_grads(h, COMP_CHUNKS)
    hand_out(1, gk, key_out)
    for h in range(2):
        query_grads(h)
    hand_out(2, gq, query_out)

    totals = [sum_chips(unit).astype(BF16) for unit in range(4)]
    done = jnp.concatenate([total[:, half(i)] for total in totals for i in range(2)], axis=0)
    rows, cols = iota((128, 128), 0), iota((128, 128), 1)
    to_owner = one_hot(cols == lax.rem(rows, 8) * 16 + lax.div(rows, 16) * 2 + lax.rem(lax.div(rows, 8), 2))
    routed = nn(to_owner, done).astype(BF16)
    for i in range(8):
        fsend[i] = routed[i * 16 : (i + 1) * 16]

    def owner_copy(i, dy, dx):
        return pltpu.make_async_remote_copy(
            fsend.at[seq_to(dy, dx)], frecv.at[s], as_sem.at[i], ar_sem.at[i],
            device_id=(c, seq_to(dy, dx)), device_id_type=MESH,
        )

    for i, (dy, dx) in enumerate(SEQ_OFFSETS):
        owner_copy(i, dy, dx).start()
    frecv[s] = fsend[s]
    place = lax.rem(lax.div(rows, 2), 8) * 16 + lax.rem(lax.div(rows, 16), 2) * 8 + lax.rem(rows, 2) * 4
    place = place + lax.div(rows, 64) * 2 + lax.rem(lax.div(rows, 32), 2)
    for i, (dy, dx) in enumerate(SEQ_OFFSETS):
        origin = lax.rem(y_lo + dy, 2) * 4 + lax.rem(x + 4 - dx, 4)
        pltpu.make_async_remote_copy(
            fsend.at[origin], frecv.at[origin], as_sem.at[i], ar_sem.at[i],
            device_id=(c, origin), device_id_type=MESH,
        ).wait_recv()
    owned = nn(one_hot(cols == place), frecv[...].reshape(128, 128)).astype(BF16)
    for i, out in ((0, pvalue_out), (1, pkey_out)):
        fout[i, :, :128] = owned[i * 64 : i * 64 + 32]
        fout[i, :, 128:] = owned[i * 64 + 32 : i * 64 + 64]
        store = pltpu.make_async_copy(fout.at[i], out, out_sem.at[3 + i])
        store.start()
        stores.append(store)

    for which in range(2):
        for h in range(2):
            for i, (dy, dx) in enumerate(SEQ_OFFSETS):
                prompt_copy(which, h, i, dy, dx).wait_send()
                forward_copy(which, h, i, dy, dx).wait_send()
    for unit in range(4):
        mate_copy(unit).wait_send()
        for i, (dy, dz) in enumerate(COMP_OFFSETS):
            chip_copy(unit, i, dy, dz).wait_send()
    for i, (dy, dx) in enumerate(SEQ_OFFSETS):
        owner_copy(i, dy, dx).wait_send()
    for store in stores:
        store.wait()


def interleaved(a):
    return a.reshape(512, 2, 2, 128).transpose(0, 2, 1, 3).reshape(2048, 128)


def by_token(a):
    return a.reshape(512, 2, 2, 128).transpose(0, 2, 1, 3).reshape(1, 512, 2, 256)


def shards(query, key, value, prompt_key, prompt_value, lam, gain, cotangent, lengths):
    vm = pltpu.VMEM
    dma = pltpu.SemaphoreType.DMA
    shape = jax.ShapeDtypeStruct
    anywhere = pl.BlockSpec(memory_space=pl.ANY)
    outs = pl.pallas_call(
        kernel,
        out_shape=[shape((2048, 128), BF16)] * 3 + [shape((32, 256), BF16)] * 2,
        in_specs=[anywhere] * 9,
        out_specs=[anywhere] * 5,
        scratch_shapes=[vm((2048, 128), BF16)] * 4
        + [vm((1024, 256), BF16)] * 2
        + [pltpu.SMEM((2,), F32), vm((2, 256), F32), pltpu.SMEM((1,), jnp.int32)]
        + [
            vm((2, 8, 2, 64, 256), BF16),
            vm((2, 1024, 256), BF16),
            vm((2, 1024, 256), BF16),
            vm((2, 512, 256), BF16),
            vm((2, 512, 256), BF16),
            vm((2, 256, 1024), BF16),
            vm((2, 256, 1024), BF16),
            vm((2, 256, 512), BF16),
            vm((2, 1024, 512), F32),
            vm((2, 1024, 512), F32),
            vm((1024, 512), F32),
            vm((2, 1024, 512), BF16),
            vm((2, 1024, 512), BF16),
            vm((2, 1024, 512), BF16),
            vm((2, 256, 512), BF16),
            vm((2, 512, 256), BF16),
            vm((2, 512, 256), BF16),
            vm((2, 512, 256), BF16),
            vm((3, 2048, 128), BF16),
            vm((4, 2, 16, 16, 256), BF16),
            vm((4, 16, 16, 256), BF16),
            vm((4, 16, 16, 256), BF16),
            vm((4, 15, 16, 256), BF16),
            vm((8, 16, 128), BF16),
            vm((8, 16, 128), BF16),
            vm((2, 32, 256), BF16),
        ]
        + [dma((9,)), dma((5,)), dma((2, 2, 7)), dma((2, 2, 7)), dma((2, 2, 7)), dma((2, 2, 7))]
        + [dma((4,)), dma((4,)), dma((4, 15)), dma((4, 15)), dma((7,)), dma((7,))],
        compiler_params=pltpu.CompilerParams(
            collective_id=0, has_side_effects=True, vmem_limit_bytes=48 * 2**20
        ),
    )(
        interleaved(query), interleaved(key), interleaved(value), interleaved(cotangent),
        prompt_key.reshape(1024, 256), prompt_value.reshape(1024, 256), lam, gain, lengths,
    )
    return (
        by_token(outs[0]), by_token(outs[1]), by_token(outs[2]),
        outs[3].reshape(2, 16, 256), outs[4].reshape(2, 16, 256),
    )


def solution(mesh):
    heads = P("comp", None, "seq", None)
    in_specs = (
        heads, heads, heads, P("seq", None, None), P("seq", None, None), P("seq"), P("seq", None), heads, P("comp"),
    )
    owners = P(("comp", "seq"), None, None)
    return jax.shard_map(
        shards, mesh=mesh, in_specs=in_specs, out_specs=(heads, heads, heads, owners, owners), check_vma=False
    )
```

time: 242 us -> 53.1 us (0.22)
  the two profiles are of different devices: /device:TPU:2 before, /device:TPU:1 now
where the time goes in v1:
time: 53.1 us; the launch traced here: 52.3 us
  Pallas kernels  40.5 us (76%)
  local copies, waits for them, and re-layouts  10.5 us (20%)
  between operations  1.31 us (2%)
    pallas_call x1, Pallas kernels, shards(): pl.pallas_call(kernel, out_shape=[shape((2048, 128), BF16)] * 3 + [shape(...  40.5 us
    unnamed x21, local copies, waits for them, and re-layouts  10.5 us

profile of v1, /device:TPU:1, one launch (start us, length us, event | category | flops | bytes accessed | tf_op | source)
XLA Modules:
  0.0 52.3 jit_solution(10291059816481112565)
XLA Ops:
  1.3 0.0 copy-start.6
  1.3 0.0 copy-start.7
  1.3 0.7 %copy-done.6 = f32[2,256]{1,0:T(2,128)S(1)} copy-done((f32[2,256]{1,0:T(2,128)S(1)}, f32[2,256]{1,0:T(2,128)}, u32[]{:S(2)}) %copy-start.6) | copy-done | bytes 2072
  2.0 0.0 copy-done.7
  2.0 0.0 copy-start
  2.0 1.0 %copy-done = bf16[1,512,2,256]{3,2,1,0:T(2,128)(2,1)S(1)} copy-done((bf16[1,512,2,256]{3,2,1,0:T(2,128)(2,1)S(1)}, bf16[1,512,2,256]{3,2,1,0:T(2,128)(2,1)}, u32[]{:S(2)}) %copy-start) | copy-done | bytes 524312
  3.0 0.0 copy-start.1
  3.0 1.0 %copy-done.1 = bf16[1,512,2,256]{3,2,1,0:T(2,128)(2,1)S(1)} copy-done((bf16[1,512,2,256]{3,2,1,0:T(2,128)(2,1)S(1)}, bf16[1,512,2,256]{3,2,1,0:T(2,128)(2,1)}, u32[]{:S(2)}) %copy-start.1) | copy-done | bytes 524312
  4.1 0.0 copy-start.2
  4.1 1.0 %copy-done.2 = bf16[1,512,2,256]{3,2,1,0:T(2,128)(2,1)S(1)} copy-done((bf16[1,512,2,256]{3,2,1,0:T(2,128)(2,1)S(1)}, bf16[1,512,2,256]{3,2,1,0:T(2,128)(2,1)}, u32[]{:S(2)}) %copy-start.2) | copy-done | bytes 524312
  5.1 0.0 copy-start.3
  5.1 1.0 %copy-done.3 = bf16[1,512,2,256]{3,2,1,0:T(2,128)(2,1)S(1)} copy-done((bf16[1,512,2,256]{3,2,1,0:T(2,128)(2,1)S(1)}, bf16[1,512,2,256]{3,2,1,0:T(2,128)(2,1)}, u32[]{:S(2)}) %copy-start.3) | copy-done | bytes 524312
  6.1 0.0 copy-start.4
  6.1 1.0 %copy-done.4 = bf16[64,16,256]{2,1,0:T(8,128)(2,1)S(1)} copy-done((bf16[64,16,256]{2,1,0:T(8,128)(2,1)S(1)}, bf16[64,16,256]{2,1,0:T(8,128)(2,1)}, u32[]{:S(2)}) %copy-start.4) | copy-done | bytes 524312
  7.2 0.0 copy-start.5
  7.2 1.0 %copy-done.5 = bf16[64,16,256]{2,1,0:T(8,128)(2,1)S(1)} copy-done((bf16[64,16,256]{2,1,0:T(8,128)(2,1)S(1)}, bf16[64,16,256]{2,1,0:T(8,128)(2,1)}, u32[]{:S(2)}) %copy-start.5) | copy-done | bytes 524312
  8.2 40.5 %shard_map.128 = (bf16[2048,128]{1,0:T(8,128)(2,1)S(1)}, bf16[2048,128]{1,0:T(8,128)(2,1)S(1)}, bf16[2048,128]{1,0:T(8,128)(2,1)S(1)}, bf16[32,256]{1,0:T(8,128)(2,1)S(1)}, bf16[32,256]{1,0:T(8,128)(2,1)S(1)}) custom-call(bf16[2048,128]{1,0:T(8,128)(2,1)S(1)} %bitcast.39, bf16[2048,128]{1,0:T(8,128)(2,1)S(1)} %bitcast.40, bf16[2048,128]{1,0:T(8,128)(2,1)S(1)} %bitcast.41, ...), custom_call_target="tpu_custom_call" | custom-call | tf_op jit(solution)/shard_map/pallas_call | solution.py:419
  48.7 0.8 %copy.27 = bf16[1,512,2,256]{3,2,1,0:T(2,128)(2,1)} copy(bf16[1,512,2,256]{3,2,1,0:T(2,128)(2,1)S(1)} %bitcast.47) | data formatting | bytes 1048576
  49.5 0.8 %copy.28 = bf16[1,512,2,256]{3,2,1,0:T(2,128)(2,1)} copy(bf16[1,512,2,256]{3,2,1,0:T(2,128)(2,1)S(1)} %bitcast.46) | data formatting | bytes 1048576
  50.3 0.8 %copy.29 = bf16[1,512,2,256]{3,2,1,0:T(2,128)(2,1)} copy(bf16[1,512,2,256]{3,2,1,0:T(2,128)(2,1)S(1)} %bitcast.45) | data formatting | bytes 1048576
  51.1 0.6 %copy.30 = bf16[2,16,256]{2,1,0:T(8,128)(2,1)} copy(bf16[2,16,256]{2,1,0:T(8,128)(2,1)S(1)} %bitcast.49) | data formatting | bytes 32768
  51.7 0.6 %copy.31 = bf16[2,16,256]{2,1,0:T(8,128)(2,1)} copy(bf16[2,16,256]{2,1,0:T(8,128)(2,1)S(1)} %bitcast.48) | data formatting | bytes 32768
Async XLA Ops:
  1.3 0.7 %copy-start.6 = (f32[2,256]{1,0:T(2,128)S(1)}, f32[2,256]{1,0:T(2,128)}, u32[]{:S(2)}) copy-start(f32[2,256]{1,0:T(2,128)} %gain_in.1) | copy-start | bytes 6148
  1.3 0.7 %copy-start.7 = (f32[2]{0:T(128)S(1)}, f32[2]{0:T(128)}, u32[]{:S(2)}) copy-start(f32[2]{0:T(128)} %lam_in.1) | copy-start | bytes 28
  2.0 1.0 %copy-start = (bf16[1,512,2,256]{3,2,1,0:T(2,128)(2,1)S(1)}, bf16[1,512,2,256]{3,2,1,0:T(2,128)(2,1)}, u32[]{:S(2)}) copy-start(bf16[1,512,2,256]{3,2,1,0:T(2,128)(2,1)} %param.9) | copy-start | bytes 1572868
  3.0 1.0 %copy-start.1 = (bf16[1,512,2,256]{3,2,1,0:T(2,128)(2,1)S(1)}, bf16[1,512,2,256]{3,2,1,0:T(2,128)(2,1)}, u32[]{:S(2)}) copy-start(bf16[1,512,2,256]{3,2,1,0:T(2,128)(2,1)} %param.10) | copy-start | bytes 1572868
  4.1 1.0 %copy-start.2 = (bf16[1,512,2,256]{3,2,1,0:T(2,128)(2,1)S(1)}, bf16[1,512,2,256]{3,2,1,0:T(2,128)(2,1)}, u32[]{:S(2)}) copy-start(bf16[1,512,2,256]{3,2,1,0:T(2,128)(2,1)} %param.11) | copy-start | bytes 1572868
  5.1 1.0 %copy-start.3 = (bf16[1,512,2,256]{3,2,1,0:T(2,128)(2,1)S(1)}, bf16[1,512,2,256]{3,2,1,0:T(2,128)(2,1)}, u32[]{:S(2)}) copy-start(bf16[1,512,2,256]{3,2,1,0:T(2,128)(2,1)} %param.16) | copy-start | bytes 1572868
  6.1 1.0 %copy-start.4 = (bf16[64,16,256]{2,1,0:T(8,128)(2,1)S(1)}, bf16[64,16,256]{2,1,0:T(8,128)(2,1)}, u32[]{:S(2)}) copy-start(bf16[64,16,256]{2,1,0:T(8,128)(2,1)} %param.12) | copy-start | bytes 1572868
  7.2 1.0 %copy-start.5 = (bf16[64,16,256]{2,1,0:T(8,128)(2,1)S(1)}, bf16[64,16,256]{2,1,0:T(8,128)(2,1)}, u32[]{:S(2)}) copy-start(bf16[64,16,256]{2,1,0:T(8,128)(2,1)} %param.13) | copy-start | bytes 1572868

commit v2 on v1

v2 whole, which is shorter than its diff:
```python
import math

import jax
import jax.numpy as jnp
from jax import lax
from jax.experimental import pallas as pl
from jax.experimental.pallas import tpu as pltpu
from jax.sharding import PartitionSpec as P

F32, BF16 = jnp.float32, jnp.bfloat16
MESH = pl.DeviceIdType.MESH
SCALE = 128**-0.5
EXPO = SCALE * math.log2(math.e)
ROWS = 32
PROMPT_CHUNKS = ((0, 256, 0), (256, 256, 0))
COMP_CHUNKS = ((512, 256, 0), (768, 256, 256))
CHUNKS = PROMPT_CHUNKS + COMP_CHUNKS
SEQ_OFFSETS = ((1, 2), (0, 2), (1, 1), (1, 3), (0, 1), (0, 3), (1, 0))
Z_OFFSETS = (4, 3, 5, 2, 6, 1, 7)
COMP_OFFSETS = tuple((dy, dz) for dz in (4, 3, 5, 2, 6, 1, 7, 0) for dy in (1, 0) if (dy, dz) != (0, 0))


def nt(a, b):
    return lax.dot_general(a, b, (((1,), (1,)), ((), ())), preferred_element_type=F32)


def nn(a, b):
    return lax.dot_general(a, b, (((1,), (0,)), ((), ())), preferred_element_type=F32)


def iota(shape, dim):
    return lax.broadcasted_iota(jnp.int32, shape, dim)


def one_hot(hits):
    return jnp.where(hits, 1.0, 0.0).astype(BF16)


def half(i):
    return slice(i * 128, (i + 1) * 128)


def fold(x, op):
    return op(x.reshape(x.shape[0] // 8, 8, x.shape[1]), axis=0)


def merge(acc, part, first, op):
    if acc is None:
        return part
    if first:
        return jnp.concatenate([acc[:, :first], op(acc[:, first:], part)], axis=1)
    return op(acc, part)


def kernel(
    query_in, key_in, value_in, cot_in, pkey_in, pvalue_in, lam_in, gain_in, length_in,
    query_out, key_out, value_out, pkey_out, pvalue_out,
    qx, kx, vx, cx, pkx, pvx, lam, gain, length,
    prompt_send, kn, vn, qn, cn, kT, vT, cT,
    s1, s2, dm, mixT, ds1, ds2, dT,
    gq, gk, gv, part, sibling, zsend, yrecv, zrecv, fsend, frecv,
    in_sem, ps_sem, pr_sem, fs_sem, fr_sem, cs_sem, cr_sem, ys_sem, yr_sem, zs_sem, zr_sem, as_sem, ar_sem,
):
    c, s = lax.axis_index("comp"), lax.axis_index("seq")
    core = lax.rem(c, 2)
    z = lax.rem(lax.div(c, 2), 8)
    y_hi = lax.div(c, 16)
    x = lax.rem(s, 4)
    y_lo = lax.div(s, 4)
    mate = (c + 1 - 2 * core, s)

    def seq_to(dy, dx):
        return lax.rem(y_lo + dy, 2) * 4 + lax.rem(x + dx, 4)

    def gather_to(dy, dx):
        comp = lax.rem(c + 16 * core, 32) if dy else c
        return comp, seq_to(dy, dx)

    def comp_at(dy, dz):
        return lax.rem(y_hi + dy, 2), lax.rem(z + dz, 8)

    def chip(dy, dz):
        other_y, other_z = comp_at(dy, dz)
        return (other_y * 8 + other_z) * 2 + core, s

    pairs = []
    for src, dst in ((pkey_in, pkx), (pvalue_in, pvx)):
        pairs += [(src.at[pl.ds(b * 256, 256)], dst.at[pl.ds(b * 256, 256)]) for b in range(4)]
    pairs += [(query_in, qx), (key_in, kx), (value_in, vx), (cot_in, cx), (gain_in, gain), (lam_in, lam), (length_in, length)]
    loads = [pltpu.make_async_copy(src, dst, in_sem.at[i]) for i, (src, dst) in enumerate(pairs)]
    for load in loads:
        load.start()

    barrier = pltpu.get_barrier_semaphore()
    greet = [mate]
    greet += [gather_to(dy, dx) for dy, dx in SEQ_OFFSETS]
    greet += [(c, seq_to(dy, dx)) for dy, dx in SEQ_OFFSETS]
    greet += [chip(dy, dz) for dy, dz in COMP_OFFSETS]
    for peer in greet:
        pl.semaphore_signal(barrier, inc=1, device_id=peer, device_id_type=MESH)

    rows, cols = iota((256, 256), 0), iota((256, 256), 1)
    by_head = one_hot(cols == lax.rem(rows, 16) * 16 + lax.div(rows, 16))

    def repack(which, packed, keep):
        for b in range(4):
            loads[which * 4 + b].wait()
            got = nn(by_head, packed[b * 256 : (b + 1) * 256, :]).astype(BF16)
            for head in range(16):
                prompt_send[which, head // 2, head % 2, b // 2, b % 2 * 16 : b % 2 * 16 + 16, :] = got[
                    head * 16 : (head + 1) * 16
                ]
        for h in range(2):
            keep[h, s, core] = prompt_send[which, s, h, core]

    def prompt_copy(which, h, dy, dx):
        return pltpu.make_async_remote_copy(
            prompt_send.at[which, seq_to(dy, dx), h, core],
            (kn, vn)[which].at[h, s, core],
            ps_sem.at[which, h],
            pr_sem.at[which, h],
            device_id=gather_to(dy, dx),
            device_id_type=MESH,
        )

    def prompt_all(which, h):
        bits = (kn, vn)[which].at[h, pl.ds(0, 7), core]
        return pltpu.make_async_remote_copy(
            bits, bits, ps_sem.at[which, h], pr_sem.at[which, h], device_id=mate, device_id_type=MESH
        )

    def forward_copy(which, h):
        bits = (kn, vn)[which].at[h, pl.ds(0, 8), core]
        return pltpu.make_async_remote_copy(
            bits, bits, fs_sem.at[which, h], fr_sem.at[which, h], device_id=mate, device_id_type=MESH
        )

    def prompt_start(which, h):
        for dy, dx in SEQ_OFFSETS:
            prompt_copy(which, h, dy, dx).start()

    def prompt_forward(which, h):
        prompt_all(which, h).wait_recv()
        forward_copy(which, h).start()

    def prompt_arrived(which, h):
        forward_copy(which, h).wait_recv()

    repack(0, pkx, kn)
    pl.semaphore_wait(barrier, len(greet))
    prompt_start(0, 0)
    repack(1, pvx, vn)
    prompt_start(1, 0)
    prompt_start(0, 1)
    prompt_start(1, 1)

    def rows_of(ref, h, first, count):
        return ref[h, first // 64 : (first + count) // 64].reshape(count, 256)

    apart = one_hot(cols == lax.rem(rows, 64) * 4 + lax.rem(lax.div(rows, 64), 2) * 2 + lax.div(rows, 128))
    together = one_hot(rows == lax.rem(cols, 64) * 4 + lax.rem(lax.div(cols, 64), 2) * 2 + lax.div(cols, 128))

    def unpack(first, second, first_to, second_to):
        for b in range(8):
            block = slice(b * 256, (b + 1) * 256)
            got = nn(apart, jnp.concatenate([first[block, :], second[block, :]], axis=1)).astype(BF16)
            for h in range(2):
                for i in range(2):
                    r = (h * 2 + i) * 64
                    t = b * 64
                    for to, val in ((first_to, got[r : r + 64, :128]), (second_to, got[r : r + 64, 128:])):
                        if to is kn or to is vn:
                            to[h, 8 + b, :, :, half(i)] = val.reshape(2, 32, 128)
                        else:
                            to[h, t : t + 64, half(i)] = val

    def turn(src, dst, h, first, last):
        for b in range(first, last, 256):
            rows = src[h, b : b + 256, :] if src is cn else rows_of(src, h, b, 256)
            dst[h, :, b : b + 256] = rows.T

    def scores(h, chunks, tops, sums):
        for k0, n, q0 in chunks:
            for i, to in ((0, s1), (1, s2)):
                keys = rows_of(kn, h, k0, n)[:, half(i)]
                some_tops, some_sums = [], []
                for q in range(q0, 512, 256):
                    val = nt(keys, qn[h, q : q + 256, half(i)])
                    if q == k0 - 512:
                        val = jnp.where(iota(val.shape, 0) <= iota(val.shape, 1), val, -1e30)
                    top = jnp.max(fold(val, jnp.max), axis=0, keepdims=True) * EXPO
                    e = jnp.exp2(val * EXPO - top)
                    to[h, k0 : k0 + n, q : q + 256] = e
                    some_tops.append(top)
                    some_sums.append(jnp.sum(fold(e, jnp.sum), axis=0, keepdims=True))
                tops[i][k0] = jnp.concatenate(some_tops, axis=1)
                sums[i][k0] = jnp.concatenate(some_sums, axis=1)

    def weights(h, tops, sums):
        found = []
        for i, factor in ((0, 1.0), (1, lam[h])):
            top, total = None, None
            for k0, _, q0 in CHUNKS:
                top = merge(top, tops[i][k0], q0, jnp.maximum)
            short = {k0: jnp.exp2(tops[i][k0] - top[:, q0:]) for k0, _, q0 in CHUNKS}
            for k0, _, q0 in CHUNKS:
                total = merge(total, sums[i][k0] * short[k0], q0, jnp.add)
            scale = factor / total
            found.append({k0: short[k0] * scale[:, q0:] for k0, _, q0 in CHUNKS})
        return found

    def forward(h, w):
        for k0, n, q0 in CHUNKS:
            for r in range(k0, k0 + n, ROWS):
                a1 = s1[h, r : r + ROWS, q0:] * w[0][k0]
                a2 = s2[h, r : r + ROWS, q0:] * w[1][k0]
                mixT[h, r : r + ROWS, q0:] = (a1 - a2).astype(BF16)
        for q in (0, 256):
            attn = nn(vT[h, :, : 768 + q], mixT[h, : 768 + q, q : q + 256])
            recip = lax.rsqrt(jnp.sum(attn * attn, axis=0, keepdims=True) * (1.0 / 256) + 1e-5)
            live = iota((1, 256), 1) + q < length[0]
            grad = jnp.where(live, cT[h, :, q : q + 256].astype(F32), 0.0) * gains[:, h : h + 1]
            inner = jnp.sum(grad * attn, axis=0, keepdims=True) * (1.0 / 256)
            dT[h, :, q : q + 256] = (recip * (grad - attn * (recip * recip * inner))).astype(BF16)

    def to_part(unit, k0, val, columns):
        for r in range(0, val.shape[0], 16):
            block = (k0 + r) // 16
            part[unit, block % 2, block // 2, :, columns] = val[r : r + 16].astype(BF16)

    def value_grads(h, chunks):
        for k0, n, q0 in chunks:
            val = nt(mixT[h, k0 : k0 + n, q0:], dT[h, :, q0:])
            if k0 < 512:
                to_part(2 * h, k0, val, slice(0, 256))
            else:
                gv[h, k0 - 512 : k0 - 512 + n, :] = val.astype(BF16)

    def key_grads(h, chunks):
        for k0, n, q0 in chunks:
            for i, ds in ((0, ds1), (1, ds2)):
                val = nn(ds[h, k0 : k0 + n, q0:], qn[h, q0:, half(i)]) * SCALE
                if k0 < 512:
                    to_part(2 * h + 1, k0, val, half(i))
                else:
                    gk[h, k0 - 512 : k0 - 512 + n, half(i)] = val.astype(BF16)

    def query_grads(h):
        for i, ds in ((0, ds1), (1, ds2)):
            for q in (0, 256):
                total = nn(kT[h, half(i), : 768 + q], ds[h, : 768 + q, q : q + 256])
                gq[h, q : q + 256, half(i)] = (total * SCALE).astype(BF16).T

    def row_sums(h, w):
        sums = [None, None]
        for k0, n, q0 in CHUNKS:
            val = nn(rows_of(vn, h, k0, n), dT[h, :, q0:])
            dm[k0 : k0 + n, q0:] = val
            for i, e in ((0, s1), (1, s2)):
                total = None
                for r in range(0, n, ROWS):
                    prod = fold(e[h, k0 + r : k0 + r + ROWS, q0:] * val[r : r + ROWS], jnp.sum)
                    total = prod if total is None else total + prod
                sums[i] = merge(sums[i], total * w[i][k0], q0, jnp.add)
        e1, e2 = [jnp.sum(total, axis=0, keepdims=True) for total in sums]
        return e1, e2 / lam[h]

    def score_grads(h, w, es, chunks):
        for k0, n, q0 in chunks:
            c1, c2 = [es[i][:, q0:] * w[i][k0] for i in range(2)]
            for r in range(k0, k0 + n, ROWS):
                bit = dm[r : r + ROWS, q0:]
                ds1[h, r : r + ROWS, q0:] = (s1[h, r : r + ROWS, q0:] * (bit * w[0][k0] - c1)).astype(BF16)
                ds2[h, r : r + ROWS, q0:] = (s2[h, r : r + ROWS, q0:] * (c2 - bit * w[1][k0])).astype(BF16)

    def mate_copy(unit):
        return pltpu.make_async_remote_copy(
            part.at[unit, 1 - core], sibling.at[unit], cs_sem.at[unit], cr_sem.at[unit],
            device_id=mate, device_id_type=MESH,
        )

    def y_copy(unit):
        return pltpu.make_async_remote_copy(
            zsend.at[unit, 1 - y_hi], yrecv.at[unit], ys_sem.at[unit], yr_sem.at[unit],
            device_id=chip(1, 0), device_id_type=MESH,
        )

    def chip_copy(unit, i, dy, dz):
        other_y, other_z = comp_at(dy, dz)
        return pltpu.make_async_remote_copy(
            zsend.at[unit, other_y, other_z], zrecv.at[unit, i], zs_sem.at[unit], zr_sem.at[unit],
            device_id=chip(dy, dz), device_id_type=MESH,
        )

    def chip_all(unit):
        bits = zrecv.at[unit, pl.ds(0, 7 if unit < 2 else 15)]
        return pltpu.make_async_remote_copy(
            bits, bits, zs_sem.at[unit], zr_sem.at[unit], device_id=mate, device_id_type=MESH
        )

    def add_mate(unit):
        mate_copy(unit).wait_recv()
        for y in range(2):
            for b in range(8):
                both = part[unit, core, y * 8 + b].astype(F32) + sibling[unit, y * 8 + b].astype(F32)
                zsend[unit, y, b] = both.astype(BF16)

    def send_y(unit):
        add_mate(unit)
        y_copy(unit).start()

    def send_z(unit):
        y_copy(unit).wait_recv()
        for b in range(8):
            both = zsend[unit, y_hi, b].astype(F32) + yrecv[unit, b].astype(F32)
            zsend[unit, y_hi, b] = both.astype(BF16)
        for i, dz in enumerate(Z_OFFSETS):
            chip_copy(unit, i, 0, dz).start()

    def send_direct(unit):
        add_mate(unit)
        for i, (dy, dz) in enumerate(COMP_OFFSETS):
            chip_copy(unit, i, dy, dz).start()

    def sum_chips(unit):
        chip_all(unit).wait_recv()
        total = zsend[unit, y_hi, z].astype(F32)
        for i in range(7 if unit < 2 else 15):
            total = total + zrecv[unit, i].astype(F32)
        return total

    loads[8].wait()
    loads[9].wait()
    unpack(qx, kx, qn, kn)
    tops, sums = ([{}, {}], [{}, {}]), ([{}, {}], [{}, {}])
    scores(0, COMP_CHUNKS, tops[0], sums[0])
    for load in loads[10:]:
        load.wait()
    unpack(vx, cx, vn, cn)
    gains = jnp.concatenate([gain[...], jnp.zeros((6, 256), F32)], axis=0).T
    scores(1, COMP_CHUNKS, tops[1], sums[1])
    for h in range(2):
        turn(cn, cT, h, 0, 512)
        turn(vn, vT, h, 512, 1024)
        turn(kn, kT, h, 512, 1024)
    prompt_forward(0, 0)
    prompt_arrived(0, 0)
    scores(0, PROMPT_CHUNKS, tops[0], sums[0])
    prompt_forward(1, 0)
    w0 = weights(0, tops[0], sums[0])
    prompt_arrived(1, 0)
    turn(vn, vT, 0, 0, 512)
    prompt_forward(0, 1)
    forward(0, w0)
    prompt_forward(1, 1)
    value_grads(0, PROMPT_CHUNKS)
    mate_copy(0).start()
    es0 = row_sums(0, w0)
    send_y(0)
    score_grads(0, w0, es0, PROMPT_CHUNKS)
    key_grads(0, PROMPT_CHUNKS)
    mate_copy(1).start()
    prompt_arrived(0, 1)
    scores(1, PROMPT_CHUNKS, tops[1], sums[1])
    score_grads(0, w0, es0, COMP_CHUNKS)
    send_y(1)
    w1 = weights(1, tops[1], sums[1])
    prompt_arrived(1, 1)
    turn(vn, vT, 1, 0, 512)
    forward(1, w1)
    send_z(0)
    value_grads(1, PROMPT_CHUNKS)
    mate_copy(2).start()
    es1 = row_sums(1, w1)
    send_z(1)
    send_direct(2)
    score_grads(1, w1, es1, PROMPT_CHUNKS)
    key_grads(1, PROMPT_CHUNKS)
    mate_copy(3).start()
    score_grads(1, w1, es1, COMP_CHUNKS)
    send_direct(3)

    def hand_out(packed, out):
        for b in range(8):
            bits = [packed[h, b * 64 : (b + 1) * 64, half(i)] for h in range(2) for i in range(2)]
            out[b * 256 : (b + 1) * 256, :] = nn(together, jnp.concatenate(bits, axis=0)).astype(BF16)

    for h in range(2):
        value_grads(h, COMP_CHUNKS)
    hand_out(gv, value_out)
    for h in range(2):
        key_grads(h, COMP_CHUNKS)
    hand_out(gk, key_out)
    for h in range(2):
        turn(kn, kT, h, 0, 512)
        query_grads(h)
    hand_out(gq, query_out)

    totals = [sum_chips(unit).astype(BF16) for unit in range(4)]
    done = jnp.concatenate([total[:, half(i)] for total in totals for i in range(2)], axis=0)
    rows, cols = iota((128, 128), 0), iota((128, 128), 1)
    to_owner = one_hot(cols == lax.rem(rows, 8) * 16 + lax.div(rows, 16) * 2 + lax.rem(lax.div(rows, 8), 2))
    routed = nn(to_owner, done).astype(BF16)
    for i in range(8):
        fsend[i] = routed[i * 16 : (i + 1) * 16]

    def owner_copy(dy, dx):
        return pltpu.make_async_remote_copy(
            fsend.at[seq_to(dy, dx)], frecv.at[s], as_sem.at[0], ar_sem.at[0],
            device_id=(c, seq_to(dy, dx)), device_id_type=MESH,
        )

    for dy, dx in SEQ_OFFSETS:
        owner_copy(dy, dx).start()
    frecv[s] = fsend[s]
    place = lax.rem(lax.div(rows, 2), 8) * 16 + lax.rem(lax.div(rows, 16), 2) * 8 + lax.rem(rows, 2) * 4
    place = place + lax.div(rows, 64) * 2 + lax.rem(lax.div(rows, 32), 2)
    bits = frecv.at[pl.ds(0, 7)]
    owner_all = pltpu.make_async_remote_copy(
        bits, bits, as_sem.at[0], ar_sem.at[0], device_id=mate, device_id_type=MESH
    )
    for which in range(2):
        for h in range(2):
            prompt_all(which, h).wait_send()
            forward_copy(which, h).wait_send()
    for unit in range(4):
        mate_copy(unit).wait_send()
        chip_all(unit).wait_send()
        if unit < 2:
            y_copy(unit).wait_send()
    owner_all.wait()
    owned = nn(one_hot(cols == place), frecv[...].reshape(128, 128)).astype(BF16)
    for i, out in ((0, pvalue_out), (1, pkey_out)):
        out[:, :128] = owned[i * 64 : i * 64 + 32]
        out[:, 128:] = owned[i * 64 + 32 : i * 64 + 64]


def writer(*refs):
    ins, outs, sem = refs[:5], refs[5:10], refs[10]
    stores = [pltpu.make_async_copy(src, dst, sem.at[i]) for i, (src, dst) in enumerate(zip(ins, outs))]
    for store in stores:
        store.start()
    for store in stores:
        store.wait()


def interleaved(a):
    return a.reshape(512, 2, 2, 128).transpose(0, 2, 1, 3).reshape(2048, 128)


def by_token(a):
    return a.reshape(512, 2, 2, 128).transpose(0, 2, 1, 3).reshape(1, 512, 2, 256)


def shards(query, key, value, prompt_key, prompt_value, lam, gain, cotangent, lengths):
    vm = pltpu.VMEM
    dma = pltpu.SemaphoreType.DMA
    shape = jax.ShapeDtypeStruct
    anywhere = pl.BlockSpec(memory_space=pltpu.HBM)
    results = [((2048, 128), BF16)] * 3 + [((32, 256), BF16)] * 2
    held = pl.pallas_call(
        kernel,
        out_shape=[vm(*result) for result in results],
        in_specs=[anywhere] * 9,
        out_specs=[pl.BlockSpec(memory_space=vm)] * 5,
        scratch_shapes=[vm((2048, 128), BF16)] * 4
        + [vm((1024, 256), BF16)] * 2
        + [pltpu.SMEM((2,), F32), vm((2, 256), F32), pltpu.SMEM((1,), jnp.int32)]
        + [
            vm((2, 8, 2, 2, 32, 256), BF16),
            vm((2, 16, 2, 32, 256), BF16),
            vm((2, 16, 2, 32, 256), BF16),
            vm((2, 512, 256), BF16),
            vm((2, 512, 256), BF16),
            vm((2, 256, 1024), BF16),
            vm((2, 256, 1024), BF16),
            vm((2, 256, 512), BF16),
            vm((2, 1024, 512), F32),
            vm((2, 1024, 512), F32),
            vm((1024, 512), F32),
            vm((2, 1024, 512), BF16),
            vm((2, 1024, 512), BF16),
            vm((2, 1024, 512), BF16),
            vm((2, 256, 512), BF16),
            vm((2, 512, 256), BF16),
            vm((2, 512, 256), BF16),
            vm((2, 512, 256), BF16),
            vm((4, 2, 16, 16, 256), BF16),
            vm((4, 16, 16, 256), BF16),
            vm((4, 2, 8, 16, 256), BF16),
            vm((2, 8, 16, 256), BF16),
            vm((4, 15, 16, 256), BF16),
            vm((8, 16, 128), BF16),
            vm((8, 16, 128), BF16),
        ]
        + [dma((15,)), dma((2, 2)), dma((2, 2)), dma((2, 2)), dma((2, 2))]
        + [dma((4,)), dma((4,)), dma((2,)), dma((2,)), dma((4,)), dma((4,)), dma((1,)), dma((1,))],
        compiler_params=pltpu.CompilerParams(
            collective_id=0, has_side_effects=True, vmem_limit_bytes=62 * 2**20
        ),
    )(
        interleaved(query), interleaved(key), interleaved(value), interleaved(cotangent),
        prompt_key.reshape(1024, 256), prompt_value.reshape(1024, 256), lam, gain, lengths,
    )
    outs = pl.pallas_call(
        writer,
        out_shape=[shape(*result) for result in results],
        in_specs=[anywhere] * 5,
        out_specs=[anywhere] * 5,
        scratch_shapes=[dma((5,))],
    )(*held)
    return (
        by_token(outs[0]), by_token(outs[1]), by_token(outs[2]),
        outs[3].reshape(2, 16, 256), outs[4].reshape(2, 16, 256),
    )


def solution(mesh):
    heads = P("comp", None, "seq", None)
    in_specs = (
        heads, heads, heads, P("seq", None, None), P("seq", None, None), P("seq"), P("seq", None), heads, P("comp"),
    )
    owners = P(("comp", "seq"), None, None)
    return jax.shard_map(
        shards, mesh=mesh, in_specs=in_specs, out_specs=(heads, heads, heads, owners, owners), check_vma=False
    )
```

time: 53.1 us -> 95.6 us (1.80)
  Pallas kernels: 40.5 us -> 90 us
  local copies, waits for them, and re-layouts: 10.5 us -> 3.57 us
    pallas_call x1 -> x2, Pallas kernels: 40.5 us -> 90 us  [the longest x1 49.8 us: shards(): pl.pallas_call(writer, out_shape=[shape(*result) for result in results],...]
    unnamed x21 -> x10, local copies, waits for them, and re-layouts: 10.5 us -> 3.57 us
where the time goes in v2:
time: 95.6 us; the launch traced here: 94.9 us
  Pallas kernels  90 us (94%)
  local copies, waits for them, and re-layouts  3.57 us (4%)
  between operations  1.3 us (1%)
    pallas_call x1, Pallas kernels, shards(): pl.pallas_call(writer, out_shape=[shape(*result) for result in results],...  49.8 us
    pallas_call x1, Pallas kernels, shards(): pl.pallas_call(kernel, out_shape=[vm(*result) for result in results], in_...  40.2 us
    unnamed x10, local copies, waits for them, and re-layouts  3.57 us

profile of v2, /device:TPU:1, one launch (start us, length us, event | category | flops | bytes accessed | tf_op | source)
XLA Modules:
  0.0 94.9 jit_solution(11009439183244395449)
XLA Ops:
  1.3 40.2 %shard_map.128 = (bf16[2048,128]{1,0:T(8,128)(2,1)S(1)}, bf16[2048,128]{1,0:T(8,128)(2,1)S(1)}, bf16[2048,128]{1,0:T(8,128)(2,1)S(1)}, bf16[32,256]{1,0:T(8,128)(2,1)S(1)}, bf16[32,256]{1,0:T(8,128)(2,1)S(1)}) custom-call(bf16[2048,128]{1,0:T(8,128)(2,1)} %bitcast.39, bf16[2048,128]{1,0:T(8,128)(2,1)} %bitcast.40, bf16[2048,128]{1,0:T(8,128)(2,1)} %bitcast.41, ...), custom_call_target="tpu_custom_call" | custom-call | tf_op jit(solution)/shard_map/pallas_call | solution.py:461
  41.5 0.0 copy-start
  41.5 0.8 copy-done
  42.3 0.0 copy-start.1
  42.3 0.8 copy-done.1
  43.1 0.0 copy-start.2
  43.1 0.8 copy-done.2
  43.9 0.0 copy-start.3
  43.9 0.6 copy-done.3
  44.5 0.0 copy-start.4
  44.5 0.6 copy-done.4
  45.1 49.8 %shard_map.129 = (bf16[2048,128]{1,0:T(8,128)(2,1)}, bf16[2048,128]{1,0:T(8,128)(2,1)}, bf16[2048,128]{1,0:T(8,128)(2,1)}, bf16[32,256]{1,0:T(8,128)(2,1)}, bf16[32,256]{1,0:T(8,128)(2,1)}) custom-call(bf16[2048,128]{1,0:T(8,128)(2,1)} %copy-done, bf16[2048,128]{1,0:T(8,128)(2,1)} %copy-done.1, bf16[2048,128]{1,0:T(8,128)(2,1)} %copy-done.2, ...), custom_call_target="tpu_custom_call" | custom-call | tf_op jit(solution)/shard_map/pallas_call | solution.py:505
Async XLA Ops:
  41.5 0.8 copy-start
  42.3 0.8 copy-start.1
  43.1 0.8 copy-start.2
  43.9 0.6 copy-start.3
  44.5 0.6 copy-start.4

commit v3 on v2

--- a/solution.py
+++ b/solution.py
@@ -17,7 +17,9 @@
 CHUNKS = PROMPT_CHUNKS + COMP_CHUNKS
 SEQ_OFFSETS = ((1, 2), (0, 2), (1, 1), (1, 3), (0, 1), (0, 3), (1, 0))
 Z_OFFSETS = (4, 3, 5, 2, 6, 1, 7)
-COMP_OFFSETS = tuple((dy, dz) for dz in (4, 3, 5, 2, 6, 1, 7, 0) for dy in (1, 0) if (dy, dz) != (0, 0))
+PLANE_OFFSETS = tuple(
+    (dh, dy, dx) for dx in (2, 1, 3, 0) for dh, dy in ((1, 1), (1, 0), (0, 1), (0, 0)) if (dh, dy, dx) != (0, 0, 0)
+)
 
 
 def nt(a, b):
@@ -58,8 +60,8 @@
     qx, kx, vx, cx, pkx, pvx, lam, gain, length,
     prompt_send, kn, vn, qn, cn, kT, vT, cT,
     s1, s2, dm, mixT, ds1, ds2, dT,
-    gq, gk, gv, part, sibling, zsend, yrecv, zrecv, fsend, frecv,
-    in_sem, ps_sem, pr_sem, fs_sem, fr_sem, cs_sem, cr_sem, ys_sem, yr_sem, zs_sem, zr_sem, as_sem, ar_sem,
+    gq, gk, gv, part, sibling, plane_send, plane_recv, z_send, z_recv,
+    in_sem, ps_sem, pr_sem, fs_sem, fr_sem, cs_sem, cr_sem, ls_sem, lr_sem, zs_sem, zr_sem,
 ):
     c, s = lax.axis_index("comp"), lax.axis_index("seq")
     core = lax.rem(c, 2)
@@ -76,12 +78,14 @@
         comp = lax.rem(c + 16 * core, 32) if dy else c
         return comp, seq_to(dy, dx)
 
-    def comp_at(dy, dz):
-        return lax.rem(y_hi + dy, 2), lax.rem(z + dz, 8)
-
-    def chip(dy, dz):
-        other_y, other_z = comp_at(dy, dz)
-        return (other_y * 8 + other_z) * 2 + core, s
+    def plane_to(dh, dy, dx):
+        return lax.rem(y_hi + dh, 2), seq_to(dy, dx)
+
+    def on_plane(y, seq):
+        return (y * 8 + z) * 2 + core, seq
+
+    def on_z(other):
+        return (y_hi * 8 + other) * 2 + core, s
 
     pairs = []
     for src, dst in ((pkey_in, pkx), (pvalue_in, pvx)):
@@ -93,9 +97,8 @@
 
     barrier = pltpu.get_barrier_semaphore()
     greet = [mate]
-    greet += [gather_to(dy, dx) for dy, dx in SEQ_OFFSETS]
-    greet += [(c, seq_to(dy, dx)) for dy, dx in SEQ_OFFSETS]
-    greet += [chip(dy, dz) for dy, dz in COMP_OFFSETS]
+    greet += [on_plane(*plane_to(*offsets)) for offsets in PLANE_OFFSETS]
+    greet += [on_z(lax.rem(z + dz, 8)) for dz in Z_OFFSETS]
     for peer in greet:
         pl.semaphore_signal(barrier, inc=1, device_id=peer, device_id_type=MESH)
 
@@ -279,55 +282,60 @@
             device_id=mate, device_id_type=MESH,
         )
 
-    def y_copy(unit):
-        return pltpu.make_async_remote_copy(
-            zsend.at[unit, 1 - y_hi], yrecv.at[unit], ys_sem.at[unit], yr_sem.at[unit],
-            device_id=chip(1, 0), device_id_type=MESH,
-        )
-
-    def chip_copy(unit, i, dy, dz):
-        other_y, other_z = comp_at(dy, dz)
-        return pltpu.make_async_remote_copy(
-            zsend.at[unit, other_y, other_z], zrecv.at[unit, i], zs_sem.at[unit], zr_sem.at[unit],
-            device_id=chip(dy, dz), device_id_type=MESH,
-        )
-
-    def chip_all(unit):
-        bits = zrecv.at[unit, pl.ds(0, 7 if unit < 2 else 15)]
+    def plane_copy(unit, offsets):
+        y, seq = plane_to(*offsets)
+        return pltpu.make_async_remote_copy(
+            plane_send.at[unit, y, seq], plane_recv.at[unit, y_hi, s], ls_sem.at[unit], lr_sem.at[unit],
+            device_id=on_plane(y, seq), device_id_type=MESH,
+        )
+
+    def plane_all(unit):
+        bits = z_recv.at[pl.ds(0, 15)]
+        return pltpu.make_async_remote_copy(
+            bits, bits, ls_sem.at[unit], lr_sem.at[unit], device_id=mate, device_id_type=MESH
+        )
+
+    def z_copy(unit, dz):
+        other = lax.rem(z + dz, 8)
+        return pltpu.make_async_remote_copy(
+            z_send.at[unit, other], z_recv.at[unit * 8 + z], zs_sem.at[unit], zr_sem.at[unit],
+            device_id=on_z(other), device_id_type=MESH,
+        )
+
+    def z_all(unit):
+        bits = z_recv.at[pl.ds(unit * 8, 7)]
         return pltpu.make_async_remote_copy(
             bits, bits, zs_sem.at[unit], zr_sem.at[unit], device_id=mate, device_id_type=MESH
         )
 
-    def add_mate(unit):
+    to_plane = one_hot(
+        cols == lax.div(rows, 128) * 128 + lax.rem(lax.div(rows, 2), 8) * 16
+        + lax.rem(lax.div(rows, 16), 8) * 2 + lax.rem(rows, 2)
+    )
+    to_z = to_plane[:128, :128]
+
+    def send_plane(unit):
         mate_copy(unit).wait_recv()
-        for y in range(2):
-            for b in range(8):
-                both = part[unit, core, y * 8 + b].astype(F32) + sibling[unit, y * 8 + b].astype(F32)
-                zsend[unit, y, b] = both.astype(BF16)
-
-    def send_y(unit):
-        add_mate(unit)
-        y_copy(unit).start()
+        both = part[unit, core].reshape(256, 256).astype(F32) + sibling[unit].reshape(256, 256).astype(F32)
+        plane_send[unit] = nn(to_plane, both.astype(BF16)).astype(BF16).reshape(2, 8, 16, 256)
+        for offsets in PLANE_OFFSETS:
+            plane_copy(unit, offsets).start()
+        plane_recv[unit, y_hi, s] = plane_send[unit, y_hi, s]
 
     def send_z(unit):
-        y_copy(unit).wait_recv()
-        for b in range(8):
-            both = zsend[unit, y_hi, b].astype(F32) + yrecv[unit, b].astype(F32)
-            zsend[unit, y_hi, b] = both.astype(BF16)
-        for i, dz in enumerate(Z_OFFSETS):
-            chip_copy(unit, i, 0, dz).start()
-
-    def send_direct(unit):
-        add_mate(unit)
-        for i, (dy, dz) in enumerate(COMP_OFFSETS):
-            chip_copy(unit, i, dy, dz).start()
-
-    def sum_chips(unit):
-        chip_all(unit).wait_recv()
-        total = zsend[unit, y_hi, z].astype(F32)
-        for i in range(7 if unit < 2 else 15):
-            total = total + zrecv[unit, i].astype(F32)
-        return total
+        plane_all(unit).wait_recv()
+        got = plane_recv[unit].reshape(2, 128, 256).astype(F32)
+        z_send[unit] = nn(to_z, (got[0] + got[1]).astype(BF16)).astype(BF16).reshape(8, 16, 256)
+        for dz in Z_OFFSETS:
+            z_copy(unit, dz).start()
+        z_recv[unit * 8 + z] = z_send[unit, z]
+
+    def sum_z(unit):
+        z_all(unit).wait_recv()
+        total = z_recv[unit * 8].astype(F32)
+        for i in range(1, 8):
+            total = total + z_recv[unit * 8 + i].astype(F32)
+        return total.astype(BF16)
 
     loads[8].wait()
     loads[9].wait()
@@ -356,29 +364,27 @@
     value_grads(0, PROMPT_CHUNKS)
     mate_copy(0).start()
     es0 = row_sums(0, w0)
-    send_y(0)
+    send_plane(0)
     score_grads(0, w0, es0, PROMPT_CHUNKS)
     key_grads(0, PROMPT_CHUNKS)
     mate_copy(1).start()
     prompt_arrived(0, 1)
     scores(1, PROMPT_CHUNKS, tops[1], sums[1])
     score_grads(0, w0, es0, COMP_CHUNKS)
-    send_y(1)
+    send_plane(1)
     w1 = weights(1, tops[1], sums[1])
     prompt_arrived(1, 1)
     turn(vn, vT, 1, 0, 512)
     forward(1, w1)
-    send_z(0)
     value_grads(1, PROMPT_CHUNKS)
     mate_copy(2).start()
     es1 = row_sums(1, w1)
-    send_z(1)
-    send_direct(2)
+    send_plane(2)
     score_grads(1, w1, es1, PROMPT_CHUNKS)
     key_grads(1, PROMPT_CHUNKS)
     mate_copy(3).start()
     score_grads(1, w1, es1, COMP_CHUNKS)
-    send_direct(3)
+    send_plane(3)
 
     def hand_out(packed, out):
         for b in range(8):
@@ -387,52 +393,32 @@
 
     for h in range(2):
         value_grads(h, COMP_CHUNKS)
-    hand_out(gv, value_out)
     for h in range(2):
         key_grads(h, COMP_CHUNKS)
-    hand_out(gk, key_out)
+    send_z(0)
     for h in range(2):
         turn(kn, kT, h, 0, 512)
         query_grads(h)
+    send_z(1)
+    hand_out(gv, value_out)
+    send_z(2)
+    hand_out(gk, key_out)
+    send_z(3)
     hand_out(gq, query_out)
 
-    totals = [sum_chips(unit).astype(BF16) for unit in range(4)]
-    done = jnp.concatenate([total[:, half(i)] for total in totals for i in range(2)], axis=0)
-    rows, cols = iota((128, 128), 0), iota((128, 128), 1)
-    to_owner = one_hot(cols == lax.rem(rows, 8) * 16 + lax.div(rows, 16) * 2 + lax.rem(lax.div(rows, 8), 2))
-    routed = nn(to_owner, done).astype(BF16)
-    for i in range(8):
-        fsend[i] = routed[i * 16 : (i + 1) * 16]
-
-    def owner_copy(dy, dx):
-        return pltpu.make_async_remote_copy(
-            fsend.at[seq_to(dy, dx)], frecv.at[s], as_sem.at[0], ar_sem.at[0],
-            device_id=(c, seq_to(dy, dx)), device_id_type=MESH,
-        )
-
-    for dy, dx in SEQ_OFFSETS:
-        owner_copy(dy, dx).start()
-    frecv[s] = fsend[s]
-    place = lax.rem(lax.div(rows, 2), 8) * 16 + lax.rem(lax.div(rows, 16), 2) * 8 + lax.rem(rows, 2) * 4
-    place = place + lax.div(rows, 64) * 2 + lax.rem(lax.div(rows, 32), 2)
-    bits = frecv.at[pl.ds(0, 7)]
-    owner_all = pltpu.make_async_remote_copy(
-        bits, bits, as_sem.at[0], ar_sem.at[0], device_id=mate, device_id_type=MESH
-    )
     for which in range(2):
         for h in range(2):
             prompt_all(which, h).wait_send()
             forward_copy(which, h).wait_send()
     for unit in range(4):
         mate_copy(unit).wait_send()
-        chip_all(unit).wait_send()
-        if unit < 2:
-            y_copy(unit).wait_send()
-    owner_all.wait()
-    owned = nn(one_hot(cols == place), frecv[...].reshape(128, 128)).astype(BF16)
+        plane_all(unit).wait_send()
+    rows, cols = iota((32, 32), 0), iota((32, 32), 1)
+    in_place = one_hot(cols == lax.rem(rows, 2) * 16 + lax.rem(lax.div(rows, 2), 8) * 2 + lax.div(rows, 16))
     for i, out in ((0, pvalue_out), (1, pkey_out)):
-        out[:, :128] = owned[i * 64 : i * 64 + 32]
-        out[:, 128:] = owned[i * 64 + 32 : i * 64 + 64]
+        out[...] = nn(in_place, jnp.concatenate([sum_z(i), sum_z(2 + i)], axis=0)).astype(BF16)
+    for unit in range(4):
+        z_all(unit).wait_send()
 
 
 def writer(*refs):
@@ -488,13 +474,12 @@
             vm((4, 2, 16, 16, 256), BF16),
             vm((4, 16, 16, 256), BF16),
             vm((4, 2, 8, 16, 256), BF16),
-            vm((2, 8, 16, 256), BF16),
-            vm((4, 15, 16, 256), BF16),
-            vm((8, 16, 128), BF16),
-            vm((8, 16, 128), BF16),
+            vm((4, 2, 8, 16, 256), BF16),
+            vm((4, 8, 16, 256), BF16),
+            vm((32, 16, 256), BF16),
         ]
         + [dma((15,)), dma((2, 2)), dma((2, 2)), dma((2, 2)), dma((2, 2))]
-        + [dma((4,)), dma((4,)), dma((2,)), dma((2,)), dma((4,)), dma((4,)), dma((1,)), dma((1,))],
+        + [dma((4,)), dma((4,)), dma((4,)), dma((4,)), dma((4,)), dma((4,))],
         compiler_params=pltpu.CompilerParams(
             collective_id=0, has_side_effects=True, vmem_limit_bytes=62 * 2**20
         ),
@@ -505,9 +490,10 @@
     outs = pl.pallas_call(
         writer,
         out_shape=[shape(*result) for result in results],
-        in_specs=[anywhere] * 5,
+        in_specs=[pl.BlockSpec(memory_space=vm)] * 5,
         out_specs=[anywhere] * 5,
         scratch_shapes=[dma((5,))],
+        compiler_params=pltpu.CompilerParams(vmem_limit_bytes=2 * 2**20),
     )(*held)
     return (
         by_token(outs[0]), by_token(outs[1]), by_token(outs[2]),

time: 95.6 us -> 38.5 us (0.40)
  Pallas kernels: 90 us -> 37.1 us
  local copies, waits for them, and re-layouts: 3.57 us -> 0 us
    pallas_call x1, Pallas kernels: 49.8 us -> 1.19 us  [shards(): pl.pallas_call(writer, out_shape=[shape(*result) for result in results],...]
    pallas_call x1, Pallas kernels: 40.2 us -> 35.9 us  [shards(): pl.pallas_call(kernel, out_shape=[vm(*result) for result in results], in_...]
    unnamed x10 -> x0, local copies, waits for them, and re-layouts: 3.57 us -> none
where the time goes in v3:
time: 38.5 us; the launch traced here: 38.4 us
  Pallas kernels  37.1 us (96%)
  between operations  1.29 us (3%)
    pallas_call x1, Pallas kernels, shards(): pl.pallas_call(kernel, out_shape=[vm(*result) for result in results], in_...  35.9 us
    pallas_call x1, Pallas kernels, shards(): pl.pallas_call(writer, out_shape=[shape(*result) for result in results],...  1.19 us

profile of v3, /device:TPU:1, one launch (start us, length us, event | category | flops | bytes accessed | tf_op | source)
XLA Modules:
  0.0 38.4 jit_solution(4315486103680508515)
XLA Ops:
  1.3 35.9 %shard_map.128 = (bf16[2048,128]{1,0:T(8,128)(2,1)S(1)}, bf16[2048,128]{1,0:T(8,128)(2,1)S(1)}, bf16[2048,128]{1,0:T(8,128)(2,1)S(1)}, bf16[32,256]{1,0:T(8,128)(2,1)S(1)}, bf16[32,256]{1,0:T(8,128)(2,1)S(1)}) custom-call(bf16[2048,128]{1,0:T(8,128)(2,1)} %bitcast.39, bf16[2048,128]{1,0:T(8,128)(2,1)} %bitcast.40, bf16[2048,128]{1,0:T(8,128)(2,1)} %bitcast.41, ...), custom_call_target="tpu_custom_call" | custom-call | tf_op jit(solution)/shard_map/pallas_call | solution.py:447
  37.2 1.2 %shard_map.129 = (bf16[2048,128]{1,0:T(8,128)(2,1)}, bf16[2048,128]{1,0:T(8,128)(2,1)}, bf16[2048,128]{1,0:T(8,128)(2,1)}, bf16[32,256]{1,0:T(8,128)(2,1)}, bf16[32,256]{1,0:T(8,128)(2,1)}) custom-call(bf16[2048,128]{1,0:T(8,128)(2,1)S(1)} %get-tuple-element.15.refs_0_, bf16[2048,128]{1,0:T(8,128)(2,1)S(1)} %get-tuple-element.16.refs_1_, ...), custom_call_target="tpu_custom_call" | custom-call | tf_op jit(solution)/shard_map/pallas_call | solution.py:490

commit v4 on v3

--- a/solution.py
+++ b/solution.py
@@ -21,6 +21,8 @@
     (dh, dy, dx) for dx in (2, 1, 3, 0) for dh, dy in ((1, 1), (1, 0), (0, 1), (0, 0)) if (dh, dy, dx) != (0, 0, 0)
 )
 
+GROUPS = ((0, 1), (1, 1), (2, 1), (3, 1))
+
 
 def nt(a, b):
     return lax.dot_general(a, b, (((1,), (1,)), ((), ())), preferred_element_type=F32)
@@ -58,8 +60,8 @@
     query_in, key_in, value_in, cot_in, pkey_in, pvalue_in, lam_in, gain_in, length_in,
     query_out, key_out, value_out, pkey_out, pvalue_out,
     qx, kx, vx, cx, pkx, pvx, lam, gain, length,
-    prompt_send, kn, vn, qn, cn, kT, vT, cT,
-    s1, s2, dm, mixT, ds1, ds2, dT,
+    prompt_send, kn, vn, qn, cn, kT, dn,
+    s1, s2, dm, mixT, ds1, ds2, dA,
     gq, gk, gv, part, sibling, plane_send, plane_recv, z_send, z_recv,
     in_sem, ps_sem, pr_sem, fs_sem, fr_sem, cs_sem, cr_sem, ls_sem, lr_sem, zs_sem, zr_sem,
 ):
@@ -92,8 +94,6 @@
         pairs += [(src.at[pl.ds(b * 256, 256)], dst.at[pl.ds(b * 256, 256)]) for b in range(4)]
     pairs += [(query_in, qx), (key_in, kx), (value_in, vx), (cot_in, cx), (gain_in, gain), (lam_in, lam), (length_in, length)]
     loads = [pltpu.make_async_copy(src, dst, in_sem.at[i]) for i, (src, dst) in enumerate(pairs)]
-    for load in loads:
-        load.start()
 
     barrier = pltpu.get_barrier_semaphore()
     greet = [mate]
@@ -101,6 +101,9 @@
     greet += [on_z(lax.rem(z + dz, 8)) for dz in Z_OFFSETS]
     for peer in greet:
         pl.semaphore_signal(barrier, inc=1, device_id=peer, device_id_type=MESH)
+
+    for load in loads:
+        load.start()
 
     rows, cols = iota((256, 256), 0), iota((256, 256), 1)
     by_head = one_hot(cols == lax.rem(rows, 16) * 16 + lax.div(rows, 16))
@@ -179,8 +182,7 @@
 
     def turn(src, dst, h, first, last):
         for b in range(first, last, 256):
-            rows = src[h, b : b + 256, :] if src is cn else rows_of(src, h, b, 256)
-            dst[h, :, b : b + 256] = rows.T
+            dst[h, :, b : b + 256] = rows_of(src, h, b, 256).T
 
     def scores(h, chunks, tops, sums):
         for k0, n, q0 in chunks:
@@ -212,19 +214,27 @@
             found.append({k0: short[k0] * scale[:, q0:] for k0, _, q0 in CHUNKS})
         return found
 
-    def forward(h, w):
+    def mix(h, w):
         for k0, n, q0 in CHUNKS:
             for r in range(k0, k0 + n, ROWS):
                 a1 = s1[h, r : r + ROWS, q0:] * w[0][k0]
                 a2 = s2[h, r : r + ROWS, q0:] * w[1][k0]
                 mixT[h, r : r + ROWS, q0:] = (a1 - a2).astype(BF16)
+
+    def tn(a, b):
+        return lax.dot_general(a, b, (((0,), (0,)), ((), ())), preferred_element_type=F32)
+
+    def wanted(h):
+        live = iota((512, 1), 0) < length[0]
+        dn[h] = jnp.where(live, cn[h].astype(F32), 0.0) * gain[h : h + 1, :]
+
+    def forward(h):
         for q in (0, 256):
-            attn = nn(vT[h, :, : 768 + q], mixT[h, : 768 + q, q : q + 256])
-            recip = lax.rsqrt(jnp.sum(attn * attn, axis=0, keepdims=True) * (1.0 / 256) + 1e-5)
-            live = iota((1, 256), 1) + q < length[0]
-            grad = jnp.where(live, cT[h, :, q : q + 256].astype(F32), 0.0) * gains[:, h : h + 1]
-            inner = jnp.sum(grad * attn, axis=0, keepdims=True) * (1.0 / 256)
-            dT[h, :, q : q + 256] = (recip * (grad - attn * (recip * recip * inner))).astype(BF16)
+            attn = tn(mixT[h, : 768 + q, q : q + 256], rows_of(vn, h, 0, 768 + q))
+            recip = lax.rsqrt(jnp.sum(attn * attn, axis=1, keepdims=True) * (1.0 / 256) + 1e-5)
+            grad = dn[h, q : q + 256, :]
+            inner = jnp.sum(grad * attn, axis=1, keepdims=True) * (1.0 / 256)
+            dA[h, q : q + 256, :] = (recip * (grad - attn * (recip * recip * inner))).astype(BF16)
 
     def to_part(unit, k0, val, columns):
         for r in range(0, val.shape[0], 16):
@@ -233,7 +243,7 @@
 
     def value_grads(h, chunks):
         for k0, n, q0 in chunks:
-            val = nt(mixT[h, k0 : k0 + n, q0:], dT[h, :, q0:])
+            val = nn(mixT[h, k0 : k0 + n, q0:], dA[h, q0:, :])
             if k0 < 512:
                 to_part(2 * h, k0, val, slice(0, 256))
             else:
@@ -257,8 +267,8 @@
     def row_sums(h, w):
         sums = [None, None]
         for k0, n, q0 in CHUNKS:
-            val = nn(rows_of(vn, h, k0, n), dT[h, :, q0:])
-            dm[k0 : k0 + n, q0:] = val
+            val = nt(rows_of(vn, h, k0, n), dA[h, q0:, :])
+            dm[h, k0 : k0 + n, q0:] = val
             for i, e in ((0, s1), (1, s2)):
                 total = None
                 for r in range(0, n, ROWS):
@@ -272,40 +282,43 @@
         for k0, n, q0 in chunks:
             c1, c2 = [es[i][:, q0:] * w[i][k0] for i in range(2)]
             for r in range(k0, k0 + n, ROWS):
-                bit = dm[r : r + ROWS, q0:]
+                bit = dm[h, r : r + ROWS, q0:]
                 ds1[h, r : r + ROWS, q0:] = (s1[h, r : r + ROWS, q0:] * (bit * w[0][k0] - c1)).astype(BF16)
                 ds2[h, r : r + ROWS, q0:] = (s2[h, r : r + ROWS, q0:] * (c2 - bit * w[1][k0])).astype(BF16)
 
-    def mate_copy(unit):
-        return pltpu.make_async_remote_copy(
-            part.at[unit, 1 - core], sibling.at[unit], cs_sem.at[unit], cr_sem.at[unit],
+    def mate_copy(first, count):
+        units = pl.ds(first, count)
+        return pltpu.make_async_remote_copy(
+            part.at[units, 1 - core], sibling.at[units], cs_sem.at[first], cr_sem.at[first],
             device_id=mate, device_id_type=MESH,
         )
 
-    def plane_copy(unit, offsets):
+    def plane_copy(first, count, offsets):
         y, seq = plane_to(*offsets)
-        return pltpu.make_async_remote_copy(
-            plane_send.at[unit, y, seq], plane_recv.at[unit, y_hi, s], ls_sem.at[unit], lr_sem.at[unit],
+        units = pl.ds(first, count)
+        return pltpu.make_async_remote_copy(
+            plane_send.at[units, y, seq], plane_recv.at[units, y_hi, s], ls_sem.at[first], lr_sem.at[first],
             device_id=on_plane(y, seq), device_id_type=MESH,
         )
 
-    def plane_all(unit):
-        bits = z_recv.at[pl.ds(0, 15)]
-        return pltpu.make_async_remote_copy(
-            bits, bits, ls_sem.at[unit], lr_sem.at[unit], device_id=mate, device_id_type=MESH
-        )
-
-    def z_copy(unit, dz):
+    def plane_all(first, count):
+        bits = part.at[pl.ds(first, count), 0, pl.ds(0, 15)]
+        return pltpu.make_async_remote_copy(
+            bits, bits, ls_sem.at[first], lr_sem.at[first], device_id=mate, device_id_type=MESH
+        )
+
+    def z_copy(first, count, dz):
         other = lax.rem(z + dz, 8)
-        return pltpu.make_async_remote_copy(
-            z_send.at[unit, other], z_recv.at[unit * 8 + z], zs_sem.at[unit], zr_sem.at[unit],
+        units = pl.ds(first, count)
+        return pltpu.make_async_remote_copy(
+            z_send.at[units, other], z_recv.at[units, z], zs_sem.at[first], zr_sem.at[first],
             device_id=on_z(other), device_id_type=MESH,
         )
 
-    def z_all(unit):
-        bits = z_recv.at[pl.ds(unit * 8, 7)]
-        return pltpu.make_async_remote_copy(
-            bits, bits, zs_sem.at[unit], zr_sem.at[unit], device_id=mate, device_id_type=MESH
+    def z_all(first, count):
+        bits = z_recv.at[pl.ds(first, count), pl.ds(0, 7)]
+        return pltpu.make_async_remote_copy(
+            bits, bits, zs_sem.at[first], zr_sem.at[first], device_id=mate, device_id_type=MESH
         )
 
     to_plane = one_hot(
@@ -314,28 +327,28 @@
     )
     to_z = to_plane[:128, :128]
 
-    def send_plane(unit):
-        mate_copy(unit).wait_recv()
-        both = part[unit, core].reshape(256, 256).astype(F32) + sibling[unit].reshape(256, 256).astype(F32)
-        plane_send[unit] = nn(to_plane, both.astype(BF16)).astype(BF16).reshape(2, 8, 16, 256)
+    def send_plane(first, count):
+        mate_copy(first, count).wait_recv()
+        for unit in range(first, first + count):
+            both = part[unit, core].reshape(256, 256).astype(F32) + sibling[unit].reshape(256, 256).astype(F32)
+            plane_send[unit] = nn(to_plane, both.astype(BF16)).astype(BF16).reshape(2, 8, 16, 256)
         for offsets in PLANE_OFFSETS:
-            plane_copy(unit, offsets).start()
-        plane_recv[unit, y_hi, s] = plane_send[unit, y_hi, s]
-
-    def send_z(unit):
-        plane_all(unit).wait_recv()
-        got = plane_recv[unit].reshape(2, 128, 256).astype(F32)
-        z_send[unit] = nn(to_z, (got[0] + got[1]).astype(BF16)).astype(BF16).reshape(8, 16, 256)
+            plane_copy(first, count, offsets).start()
+        for unit in range(first, first + count):
+            plane_recv[unit, y_hi, s] = plane_send[unit, y_hi, s]
+
+    def send_z(first, count):
+        plane_all(first, count).wait_recv()
+        for unit in range(first, first + count):
+            got = plane_recv[unit].reshape(2, 128, 256).astype(F32)
+            z_send[unit] = nn(to_z, (got[0] + got[1]).astype(BF16)).astype(BF16).reshape(8, 16, 256)
         for dz in Z_OFFSETS:
-            z_copy(unit, dz).start()
-        z_recv[unit * 8 + z] = z_send[unit, z]
+            z_copy(first, count, dz).start()
+        for unit in range(first, first + count):
+            z_recv[unit, z] = z_send[unit, z]
 
     def sum_z(unit):
-        z_all(unit).wait_recv()
-        total = z_recv[unit * 8].astype(F32)
-        for i in range(1, 8):
-            total = total + z_recv[unit * 8 + i].astype(F32)
-        return total.astype(BF16)
+        return jnp.sum(z_recv[unit].astype(F32), axis=0).astype(BF16)
 
     loads[8].wait()
     loads[9].wait()
@@ -345,46 +358,44 @@
     for load in loads[10:]:
         load.wait()
     unpack(vx, cx, vn, cn)
-    gains = jnp.concatenate([gain[...], jnp.zeros((6, 256), F32)], axis=0).T
     scores(1, COMP_CHUNKS, tops[1], sums[1])
     for h in range(2):
-        turn(cn, cT, h, 0, 512)
-        turn(vn, vT, h, 512, 1024)
+        wanted(h)
         turn(kn, kT, h, 512, 1024)
     prompt_forward(0, 0)
+    prompt_forward(1, 0)
     prompt_arrived(0, 0)
     scores(0, PROMPT_CHUNKS, tops[0], sums[0])
-    prompt_forward(1, 0)
     w0 = weights(0, tops[0], sums[0])
+    mix(0, w0)
+    prompt_forward(0, 1)
     prompt_arrived(1, 0)
-    turn(vn, vT, 0, 0, 512)
-    prompt_forward(0, 1)
-    forward(0, w0)
+    forward(0)
+    value_grads(0, PROMPT_CHUNKS)
+    mate_copy(0, 1).start()
     prompt_forward(1, 1)
-    value_grads(0, PROMPT_CHUNKS)
-    mate_copy(0).start()
     es0 = row_sums(0, w0)
-    send_plane(0)
     score_grads(0, w0, es0, PROMPT_CHUNKS)
     key_grads(0, PROMPT_CHUNKS)
-    mate_copy(1).start()
+    mate_copy(1, 1).start()
     prompt_arrived(0, 1)
     scores(1, PROMPT_CHUNKS, tops[1], sums[1])
-    score_grads(0, w0, es0, COMP_CHUNKS)
-    send_plane(1)
     w1 = weights(1, tops[1], sums[1])
+    send_plane(0, 1)
+    mix(1, w1)
+    send_plane(1, 1)
     prompt_arrived(1, 1)
-    turn(vn, vT, 1, 0, 512)
-    forward(1, w1)
+    forward(1)
     value_grads(1, PROMPT_CHUNKS)
-    mate_copy(2).start()
+    mate_copy(2, 1).start()
     es1 = row_sums(1, w1)
-    send_plane(2)
     score_grads(1, w1, es1, PROMPT_CHUNKS)
     key_grads(1, PROMPT_CHUNKS)
-    mate_copy(3).start()
+    mate_copy(3, 1).start()
+    send_plane(2, 1)
     score_grads(1, w1, es1, COMP_CHUNKS)
-    send_plane(3)
+    send_plane(3, 1)
+    score_grads(0, w0, es0, COMP_CHUNKS)
 
     def hand_out(packed, out):
         for b in range(8):
@@ -395,30 +406,33 @@
         value_grads(h, COMP_CHUNKS)
     for h in range(2):
         key_grads(h, COMP_CHUNKS)
-    send_z(0)
     for h in range(2):
         turn(kn, kT, h, 0, 512)
         query_grads(h)
-    send_z(1)
+    send_z(0, 1)
     hand_out(gv, value_out)
-    send_z(2)
+    send_z(1, 1)
     hand_out(gk, key_out)
-    send_z(3)
     hand_out(gq, query_out)
+    send_z(2, 1)
+    send_z(3, 1)
 
     for which in range(2):
         for h in range(2):
             prompt_all(which, h).wait_send()
             forward_copy(which, h).wait_send()
-    for unit in range(4):
-        mate_copy(unit).wait_send()
-        plane_all(unit).wait_send()
+    for group in GROUPS:
+        mate_copy(*group).wait_send()
+        plane_all(*group).wait_send()
     rows, cols = iota((32, 32), 0), iota((32, 32), 1)
     in_place = one_hot(cols == lax.rem(rows, 2) * 16 + lax.rem(lax.div(rows, 2), 8) * 2 + lax.div(rows, 16))
-    for i, out in ((0, pvalue_out), (1, pkey_out)):
-        out[...] = nn(in_place, jnp.concatenate([sum_z(i), sum_z(2 + i)], axis=0)).astype(BF16)
-    for unit in range(4):
-        z_all(unit).wait_send()
+    z_all(0, 1).wait()
+    z_all(2, 1).wait()
+    pvalue_out[...] = nn(in_place, jnp.concatenate([sum_z(0), sum_z(2)], axis=0)).astype(BF16)
+    z_all(1, 1).wait()
+    first_key = sum_z(1)
+    z_all(3, 1).wait()
+    pkey_out[...] = nn(in_place, jnp.concatenate([first_key, sum_z(3)], axis=0)).astype(BF16)
 
 
 def writer(*refs):
@@ -459,15 +473,14 @@
             vm((2, 512, 256), BF16),
             vm((2, 512, 256), BF16),
             vm((2, 256, 1024), BF16),
-            vm((2, 256, 1024), BF16),
-            vm((2, 256, 512), BF16),
+            vm((2, 512, 256), F32),
             vm((2, 1024, 512), F32),
             vm((2, 1024, 512), F32),
-            vm((1024, 512), F32),
+            vm((2, 1024, 512), F32),
             vm((2, 1024, 512), BF16),
             vm((2, 1024, 512), BF16),
             vm((2, 1024, 512), BF16),
-            vm((2, 256, 512), BF16),
+            vm((2, 512, 256), BF16),
             vm((2, 512, 256), BF16),
             vm((2, 512, 256), BF16),
             vm((2, 512, 256), BF16),
@@ -476,7 +489,7 @@
             vm((4, 2, 8, 16, 256), BF16),
             vm((4, 2, 8, 16, 256), BF16),
             vm((4, 8, 16, 256), BF16),
-            vm((32, 16, 256), BF16),
+            vm((4, 8, 16, 256), BF16),
         ]
         + [dma((15,)), dma((2, 2)), dma((2, 2)), dma((2, 2)), dma((2, 2))]
         + [dma((4,)), dma((4,)), dma((4,)), dma((4,)), dma((4,)), dma((4,))],

time: 38.5 us -> 37.4 us (0.971)
  Pallas kernels: 37.1 us -> 36 us
    pallas_call x1, Pallas kernels: 35.9 us -> 34.8 us  [shards(): pl.pallas_call(kernel, out_shape=[vm(*result) for result in results], in_...]
where the time goes in v4:
time: 37.4 us; the launch traced here: 37.3 us
  Pallas kernels  36 us (96%)
  between operations  1.29 us (3%)
    pallas_call x1, Pallas kernels, shards(): pl.pallas_call(kernel, out_shape=[vm(*result) for result in results], in_...  34.8 us
    pallas_call x1, Pallas kernels, shards(): pl.pallas_call(writer, out_shape=[shape(*result) for result in results],...  1.19 us

profile of v4, /device:TPU:1, one launch (start us, length us, event | category | flops | bytes accessed | tf_op | source)
XLA Modules:
  0.0 37.3 jit_solution(10672824596483227678)
XLA Ops:
  1.3 34.8 %shard_map.128 = (bf16[2048,128]{1,0:T(8,128)(2,1)S(1)}, bf16[2048,128]{1,0:T(8,128)(2,1)S(1)}, bf16[2048,128]{1,0:T(8,128)(2,1)S(1)}, bf16[32,256]{1,0:T(8,128)(2,1)S(1)}, bf16[32,256]{1,0:T(8,128)(2,1)S(1)}) custom-call(bf16[2048,128]{1,0:T(8,128)(2,1)} %bitcast.39, bf16[2048,128]{1,0:T(8,128)(2,1)} %bitcast.40, bf16[2048,128]{1,0:T(8,128)(2,1)} %bitcast.41, ...), custom_call_target="tpu_custom_call" | custom-call | tf_op jit(solution)/shard_map/pallas_call | solution.py:461
  36.1 1.2 %shard_map.129 = (bf16[2048,128]{1,0:T(8,128)(2,1)}, bf16[2048,128]{1,0:T(8,128)(2,1)}, bf16[2048,128]{1,0:T(8,128)(2,1)}, bf16[32,256]{1,0:T(8,128)(2,1)}, bf16[32,256]{1,0:T(8,128)(2,1)}) custom-call(bf16[2048,128]{1,0:T(8,128)(2,1)S(1)} %get-tuple-element.15.refs_0_, bf16[2048,128]{1,0:T(8,128)(2,1)S(1)} %get-tuple-element.16.refs_1_, ...), custom_call_target="tpu_custom_call" | custom-call | tf_op jit(solution)/shard_map/pallas_call | solution.py:503

commit v5 on v4

--- a/solution.py
+++ b/solution.py
@@ -157,8 +157,6 @@
     prompt_start(0, 0)
     repack(1, pvx, vn)
     prompt_start(1, 0)
-    prompt_start(0, 1)
-    prompt_start(1, 1)
 
     def rows_of(ref, h, first, count):
         return ref[h, first // 64 : (first + count) // 64].reshape(count, 256)
@@ -353,6 +351,8 @@
     loads[8].wait()
     loads[9].wait()
     unpack(qx, kx, qn, kn)
+    prompt_start(0, 1)
+    prompt_start(1, 1)
     tops, sums = ([{}, {}], [{}, {}]), ([{}, {}], [{}, {}])
     scores(0, COMP_CHUNKS, tops[0], sums[0])
     for load in loads[10:]:

time: 37.4 us -> 37.5 us (level)
  no operation moved by 1% of the time
where the time goes in v5:
time: 37.5 us; the launch traced here: 37.4 us
  Pallas kernels  36.1 us (96%)
  between operations  1.29 us (3%)
    pallas_call x1, Pallas kernels, shards(): pl.pallas_call(kernel, out_shape=[vm(*result) for result in results], in_...  34.9 us
    pallas_call x1, Pallas kernels, shards(): pl.pallas_call(writer, out_shape=[shape(*result) for result in results],...  1.19 us

profile of v5, /device:TPU:1, one launch (start us, length us, event | category | flops | bytes accessed | tf_op | source)
XLA Modules:
  0.0 37.4 jit_solution(9015587358012383153)
XLA Ops:
  1.3 34.9 %shard_map.128 = (bf16[2048,128]{1,0:T(8,128)(2,1)S(1)}, bf16[2048,128]{1,0:T(8,128)(2,1)S(1)}, bf16[2048,128]{1,0:T(8,128)(2,1)S(1)}, bf16[32,256]{1,0:T(8,128)(2,1)S(1)}, bf16[32,256]{1,0:T(8,128)(2,1)S(1)}) custom-call(bf16[2048,128]{1,0:T(8,128)(2,1)} %bitcast.39, bf16[2048,128]{1,0:T(8,128)(2,1)} %bitcast.40, bf16[2048,128]{1,0:T(8,128)(2,1)} %bitcast.41, ...), custom_call_target="tpu_custom_call" | custom-call | tf_op jit(solution)/shard_map/pallas_call | solution.py:461
  36.2 1.2 %shard_map.129 = (bf16[2048,128]{1,0:T(8,128)(2,1)}, bf16[2048,128]{1,0:T(8,128)(2,1)}, bf16[2048,128]{1,0:T(8,128)(2,1)}, bf16[32,256]{1,0:T(8,128)(2,1)}, bf16[32,256]{1,0:T(8,128)(2,1)}) custom-call(bf16[2048,128]{1,0:T(8,128)(2,1)S(1)} %get-tuple-element.15.refs_0_, bf16[2048,128]{1,0:T(8,128)(2,1)S(1)} %get-tuple-element.16.refs_1_, ...), custom_call_target="tpu_custom_call" | custom-call | tf_op jit(solution)/shard_map/pallas_call | solution.py:503
